TPU v7x, 32 devices: a whole 2x2x4 slice. The times are simulated.
32 devices in a mesh: grp: 4 (over z), ep: 8 (over y, x, core).
Axes of the slice: x: 2, y: 2, z: 4, core: 2. Of those that a mesh axis runs over, the one named last changes fastest.
Arguments:
- tokens: bfloat16 [512, 4096], P('grp', 'ep'), may hold values from -6 to 6
- grad_out: bfloat16 [512, 4096], P('grp', 'ep'), may hold values from -1.5 to 1.5
- routes: int32 [512, 2], P('grp'), may hold values from 0 to 1, as said below
- route_weights: float32 [512, 2], P('grp'), may hold values from 0.1 to 1
- gate_weight: bfloat16 [4, 384, 4096], P('grp'), may hold values from -0.09375 to 0.09375
- up_weight: bfloat16 [4, 384, 4096], P('grp'), may hold values from -0.09375 to 0.09375
- down_weight: bfloat16 [4, 384, 4096], P('grp'), may hold values from -0.21875 to 0.21875
Outputs:
- grad_tokens: bfloat16 [512, 4096], P('grp', 'ep')
- grad_gates: float32 [512, 2], P('grp')
Inputs may be any that keep to these rules, and one draw needn't show every extreme that they name: The 2 routes of a token name different experts. Among the routes of the 128 tokens of one group, no expert is named more than 128 times; in every draw one expert is named exactly 128 times in every group.
All inputs are finite; a program needn't handle non-finite values.
Results may differ from a plain program's by a relative error of at most 0.0065.
Values may be sent and summed in bfloat16 or wider, within the bound.
No kernel may reach another device: no remote copies, remote signals or barrier semaphores. Data moves between devices by JAX's collectives and lax.ppermute only.
A program may use at most 64 MiB of HBM per device.

v0:
```python
import jax
import jax.numpy as jnp
from jax import lax
from jax.sharding import PartitionSpec as P

TOP = 2


def from_behind(value, axis, steps):
    count = lax.axis_size(axis)
    pairs = [(source, (source + steps) % count) for source in range(count)]
    return lax.ppermute(value, axis, pairs)


def half_terms(rows_in, rows_back, gate_half, up_half, down_half):
    contract = (((1,), (1,)), ((), ()))
    gate_pre = lax.dot_general(rows_in, gate_half, contract, preferred_element_type=jnp.float32)
    up_pre = lax.dot_general(rows_in, up_half, contract, preferred_element_type=jnp.float32)
    back_proj = lax.dot_general(rows_back, down_half, contract, preferred_element_type=jnp.float32)
    sigmoid_gate = jax.nn.sigmoid(gate_pre)
    active = gate_pre * sigmoid_gate
    hidden = (active * up_pre).astype(jnp.bfloat16)
    hidden = lax.optimization_barrier(hidden)
    inner_sum = jnp.sum(hidden.astype(jnp.float32) * back_proj, axis=1)
    grad_gate_pre = (
        back_proj * up_pre * sigmoid_gate * (1.0 + gate_pre * (1.0 - sigmoid_gate))
    ).astype(jnp.bfloat16)
    grad_up_pre = (back_proj * active).astype(jnp.bfloat16)
    partial_value = jnp.dot(grad_gate_pre, gate_half, preferred_element_type=jnp.float32)
    partial_value = partial_value + jnp.dot(
        grad_up_pre, up_half, preferred_element_type=jnp.float32
    )
    return (inner_sum, partial_value.astype(jnp.bfloat16))


def on_device(tokens, grad_out, routes, route_weights, gate_weight, up_weight, down_weight):
    group_count = lax.axis_size("grp")
    rank_count = lax.axis_size("ep")
    pair_count = group_count // 2
    local_rank = lax.axis_index("ep")
    group_tokens, feat_width = tokens.shape
    full_width = feat_width * rank_count
    per_device = group_tokens // rank_count
    half_cap = (per_device * TOP + 2 * pair_count - 1) // (2 * pair_count)
    slot_total = group_count * rank_count * half_cap
    flat_expert = routes.reshape(-1)
    route_total = flat_expert.shape[0]
    onehot = (flat_expert[:, None] == jnp.arange(pair_count, dtype=jnp.int32)[None, :]).astype(
        jnp.int32
    )
    running = jnp.cumsum(onehot, axis=0)
    order_rank = jnp.sum((running - 1) * onehot, axis=1)
    parity = order_rank % 2
    dest_rank = order_rank // 2 % rank_count
    position = order_rank // (2 * rank_count)
    dest_group = parity * pair_count + flat_expert
    slot_index = (dest_group * rank_count + dest_rank) * half_cap + position
    source_token = (
        jnp.zeros((slot_total,), jnp.int32)
        .at[slot_index]
        .set(jnp.arange(route_total, dtype=jnp.int32) // TOP)
    )
    filled = jnp.zeros((slot_total,), jnp.bool_).at[slot_index].set(True)

    def pack_rows(values):
        picked = jnp.where(filled[:, None], values[source_token], jnp.zeros((), values.dtype))
        return picked.reshape(group_count, rank_count, half_cap, feat_width)

    send_in = pack_rows(tokens)
    send_back = pack_rows(grad_out)
    own_in, own_back = (
        lax.all_to_all(
            lax.all_to_all(send_in, "grp", split_axis=0, concat_axis=0, tiled=True),
            "ep",
            split_axis=1,
            concat_axis=3,
            tiled=True,
        ),
        lax.all_to_all(
            lax.all_to_all(send_back, "grp", split_axis=0, concat_axis=0, tiled=True),
            "ep",
            split_axis=1,
            concat_axis=3,
            tiled=True,
        ),
    )
    other_in, other_back = from_behind((own_in, own_back), "grp", pair_count)
    rows_in = jnp.concatenate(
        [own_in.reshape(-1, full_width), other_in.reshape(-1, full_width)], axis=0
    )
    rows_back = jnp.concatenate(
        [own_back.reshape(-1, full_width), other_back.reshape(-1, full_width)], axis=0
    )
    inner_sum, partial_value = half_terms(
        rows_in, rows_back, gate_weight[0], up_weight[0], down_weight[0]
    )
    half_rows = group_count * half_cap
    own_part = partial_value[:half_rows].reshape(group_count, 1, half_cap, full_width)
    other_part = partial_value[half_rows:].reshape(group_count, 1, half_cap, full_width)
    own_inner = inner_sum[:half_rows].reshape(group_count, half_cap)
    other_inner = inner_sum[half_rows:].reshape(group_count, half_cap)
    returned = from_behind(other_part, "grp", pair_count)
    pair_sum = (own_part.astype(jnp.float32) + returned.astype(jnp.float32)).astype(jnp.bfloat16)
    arrived = lax.all_to_all(
        lax.all_to_all(pair_sum, "grp", split_axis=0, concat_axis=0, tiled=True),
        "ep",
        split_axis=3,
        concat_axis=1,
        tiled=True,
    )
    summed = arrived.astype(jnp.float32)
    inner_first, inner_second = (
        lax.all_to_all(own_inner, "grp", split_axis=0, concat_axis=0, tiled=True),
        lax.all_to_all(other_inner, "grp", split_axis=0, concat_axis=0, tiled=True),
    )
    inner_total = inner_first + jnp.roll(inner_second, pair_count, axis=0)
    per_route = summed.reshape(slot_total, feat_width)[slot_index]
    weighted = per_route.reshape(group_tokens, TOP, feat_width) * route_weights[:, :, None]
    grad_tokens = jnp.sum(weighted, axis=1).astype(jnp.bfloat16)
    on_rank = dest_rank == local_rank
    gate_part = jnp.where(on_rank, inner_total[dest_group, position], jnp.zeros((), jnp.float32))
    grad_gates = lax.psum(gate_part.reshape(group_tokens, TOP), "ep")
    return (grad_tokens, grad_gates)


def solution(mesh):
    placed = (
        P("grp", "ep"),
        P("grp", "ep"),
        P("grp", None),
        P("grp", None),
        P("grp", None, None),
        P("grp", None, None),
        P("grp", None, None),
    )
    return jax.shard_map(
        on_device,
        mesh=mesh,
        in_specs=placed,
        out_specs=(P("grp", "ep"), P("grp", None)),
        check_vma=False,
    )
```

profile of v0, /device:TPU:0, one launch (start us, length us, event | category | flops | bytes accessed | tf_op | source)
XLA Modules:
  0.0 184.1 jit_solution(12655074698176584062)
XLA Ops:
  0.6 0.0 copy-start
  0.7 1.0 copy.46
  1.6 0.1 eq.39
  1.7 0.1 eq.35
  1.9 0.1 reshape.307
  2.1 0.6 reduce-window.6
  2.7 0.2 slice_reduce_fusion
  2.9 0.2 reduce-window.9
  3.1 0.1 add_bitcast_fusion
  3.2 1.4 scatter_custom_fusion.1
  4.7 2.1 %gather_fusion = bf16[256,512]{1,0:T(8,128)(2,1)S(1)} fusion(bf16[128,512]{1,0:T(8,128)(2,1)} %param.8, s32[1024]{0:T(1024)S(1)} %pad_clamp_fusion.1), kind=kCustom, calls=%fused_computation | custom fusion | bytes 525312 | tf_op jit(solution)/shard_map/gather | solution.py:66
  6.8 1.8 gather_fusion.1
  8.7 1.5 scatter_custom_fusion
  10.1 0.1 broadcast_in_dim.43
  10.2 1.8 broadcast_select_fusion.1
  12.0 15.0 %all_to_all.81 = bf16[4,8,8,512]{3,2,1,0:T(8,128)(2,1)S(1)} all-to-all(bf16[4,8,8,512]{3,2,1,0:T(8,128)(2,1)S(1)} %get-tuple-element.14), channel_id=1, replica_groups=mesh['grp'=4,'ep'=8] {'grp'}, dimensions={0} | all-to-all | bytes 524288 | tf_op jit(solution)/shard_map/all_to_all | solution.py:73
  27.0 10.5 %all_to_all.82 = bf16[4,8,8,512]{3,2,0,1:T(8,128)(2,1)S(1)} all-to-all(bf16[4,8,8,512]{3,2,0,1:T(8,128)(2,1)S(1)} %copy.52), channel_id=1, replica_groups=mesh['grp'=4,'ep'=8] {'ep'}, dimensions={1} | all-to-all | bytes 524288 | tf_op jit(solution)/shard_map/all_to_all | solution.py:72
  37.5 4.0 %all-to-all-start = ((bf16[4,8,8,512]{3,2,1,0:T(8,128)(2,1)}), bf16[4,8,8,512]{3,2,1,0:T(8,128)(2,1)}, u32[]{:S(2)}, u32[]{:S(2)}) async-start(bf16[4,8,8,512]{3,2,1,0:T(8,128)(2,1)} %get-tuple-element.13), calls=%async_computation | async-start | bytes 524288 | tf_op jit(solution)/shard_map/all_to_all | solution.py:80
  41.5 0.7 copy.64
  42.2 2.9 %collective-permute-start.1 = (bf16[4,1,8,4096]{3,2,0,1:T(8,128)(2,1)}, bf16[4,1,8,4096]{3,2,0,1:T(8,128)(2,1)}, u32[]{:S(2)}, u32[]{:S(2)}) collective-permute-start(bf16[4,1,8,4096]{3,2,0,1:T(8,128)(2,1)} %bitcast.38), channel_id=1, source_target_pairs={{0,16},{8,24},{16,0},{24,8},{1,17},{9,25},{17,1},{25,9},{2,18},{10... | collective-permute-start | bytes 786440 | tf_op jit(solution)/shard_map/ppermute | solution.py:12
  45.1 11.7 %all-to-all-done = bf16[4,8,8,512]{3,2,1,0:T(8,128)(2,1)} async-done(((bf16[4,8,8,512]{3,2,1,0:T(8,128)(2,1)}), bf16[4,8,8,512]{3,2,1,0:T(8,128)(2,1)}, u32[]{:S(2)}, u32[]{:S(2)}) %all-to-all-start) | async-done | bytes 262176 | tf_op jit(solution)/shard_map/all_to_all | solution.py:80
  56.8 1.7 copy.49
  58.5 4.1 %all-to-all-start.1 = ((bf16[4,8,8,512]{3,2,0,1:T(8,128)(2,1)}), bf16[4,8,8,512]{3,2,0,1:T(8,128)(2,1)}, u32[]{:S(2)}, u32[]{:S(2)}) async-start(bf16[4,8,8,512]{3,2,0,1:T(8,128)(2,1)} %copy.49), calls=%async_computation.1 | async-start | bytes 524288 | tf_op jit(solution)/shard_map/all_to_all | solution.py:79
  62.6 0.1 reduce_sum.34
  62.7 0.1 copy.71
  62.9 0.1 copy.67
  63.0 6.5 %all-to-all-done.1 = bf16[4,8,8,512]{3,2,0,1:T(8,128)(2,1)} async-done(((bf16[4,8,8,512]{3,2,0,1:T(8,128)(2,1)}), bf16[4,8,8,512]{3,2,0,1:T(8,128)(2,1)}, u32[]{:S(2)}, u32[]{:S(2)}) %all-to-all-start.1) | async-done | bytes 262176 | tf_op jit(solution)/shard_map/all_to_all | solution.py:79
  69.5 1.0 copy.63
  70.5 0.1 collective-permute-start
  70.6 1.1 copy.72
  71.7 0.1 copy.66
  71.8 3.2 %fusion.3 = f32[64,384]{1,0:T(8,128)S(1)} fusion(bf16[1,384,4096]{2,1,0:T(8,128)(2,1)} %param.11, bf16[32,4096]{1,0:T(8,128)(2,1)} %bitcast.13, bf16[32,4096]{1,0:T(8,128)(2,1)S(1)} %bitcast.83), kind=kOutput, calls=%fused_computation.10 | convolution fusion | flops 202375168 | bytes 3768320 | tf_op jit(solution)/shard_map/dot_general | solution.py:17
  75.0 2.2 %multiply_convert_fusion = (bf16[64,384]{1,0:T(8,128)(2,1)S(1)}, f32[64,384]{1,0:T(8,128)S(1)}) fusion(f32[64,384]{1,0:T(8,128)S(1)} %fusion.3, bf16[1,384,4096]{2,1,0:T(8,128)(2,1)S(1)} %copy-done, bf16[32,4096]{1,0:T(8,128)(2,1)} %bitcast.13, bf16[32,4096]{1,0:T(8,128)(2,1)S(1)} %bitcast.84), kind=kOutput, calls=%fused_computation.31 | convolution fusion | flops 202522624 | bytes 3915776 | tf_op jit(solution)/shard_map/dot_general | solution.py:18
  77.2 5.8 %collective-permute-done = bf16[4,1,8,4096]{3,2,0,1:T(8,128)(2,1)S(1)} collective-permute-done((bf16[4,1,8,4096]{3,2,0,1:T(8,128)(2,1)S(1)}, bf16[4,1,8,4096]{3,2,0,1:T(8,128)(2,1)S(1)}, u32[]{:S(2)}, u32[]{:S(2)}) %collective-permute-start) | collective-permute-done | bytes 262176 | tf_op jit(solution)/shard_map/ppermute | solution.py:12
  83.1 1.1 fusion.8
  84.2 0.7 fusion.1
  84.9 0.7 fusion
  85.6 0.8 copy-done.4
  86.4 0.7 slice_bitcast_fusion
  87.1 0.1 multiply_reduce_fusion.1
  87.2 0.1 fusion.43
  87.3 0.7 all_to_all.71
  88.0 4.3 %all-to-all-start.7 = ((f32[4,1,8]{2,1,0:T(1,128)}), f32[4,1,8]{2,1,0:T(1,128)S(1)}, u32[]{:S(2)}, u32[]{:S(2)}) async-start(f32[4,1,8]{2,1,0:T(1,128)} %bitcast.25), calls=%async_computation.7 | async-start | bytes 4096 | tf_op jit(solution)/shard_map/all_to_all | solution.py:114
  92.2 0.7 copy.59
  93.0 0.7 all_to_all.68
  93.6 8.2 %all-to-all-done.7 = f32[4,1,8]{2,1,0:T(1,128)S(1)} async-done(((f32[4,1,8]{2,1,0:T(1,128)}), f32[4,1,8]{2,1,0:T(1,128)S(1)}, u32[]{:S(2)}, u32[]{:S(2)}) %all-to-all-start.7) | async-done | bytes 160 | tf_op jit(solution)/shard_map/all_to_all | solution.py:114
  101.8 3.2 %all-to-all-start.6 = ((f32[4,1,8]{2,1,0:T(1,128)}), f32[4,1,8]{2,1,0:T(1,128)S(1)}, u32[]{:S(2)}, u32[]{:S(2)}) async-start(f32[4,1,8]{2,1,0:T(1,128)} %bitcast.23), calls=%async_computation.6 | async-start | bytes 4096 | tf_op jit(solution)/shard_map/all_to_all | solution.py:113
  105.1 1.7 fusion.13
  106.8 3.6 %all-to-all-done.6 = f32[4,1,8]{2,1,0:T(1,128)S(1)} async-done(((f32[4,1,8]{2,1,0:T(1,128)}), f32[4,1,8]{2,1,0:T(1,128)S(1)}, u32[]{:S(2)}, u32[]{:S(2)}) %all-to-all-start.6) | async-done | bytes 160 | tf_op jit(solution)/shard_map/all_to_all | solution.py:113
  110.4 3.4 %all-to-all-start.4 = ((bf16[4,1,8,4096]{3,2,1,0:T(8,128)(2,1)}), bf16[4,1,8,4096]{3,2,1,0:T(8,128)(2,1)S(1)}, u32[]{:S(2)}, u32[]{:S(2)}) async-start(bf16[4,1,8,4096]{3,2,1,0:T(8,128)(2,1)} %fusion.13), calls=%async_computation.4 | async-start | bytes 524288 | tf_op jit(solution)/shard_map/all_to_all | solution.py:105
  113.9 2.4 %gather_fusion.3 = f32[256]{0:T(256)S(1)} fusion(f32[4,8]{1,0:T(4,128)S(1)} %maximum_add_fusion, s32[256]{0:T(256)S(1)} %bitcast.80), kind=kCustom, calls=%fused_computation.3 | custom fusion | bytes 4096 | tf_op jit(solution)/shard_map/gather | solution.py:121
  116.3 0.1 gather.24
  116.4 5.6 %all-to-all-done.4 = bf16[4,1,8,4096]{3,2,1,0:T(8,128)(2,1)S(1)} async-done(((bf16[4,1,8,4096]{3,2,1,0:T(8,128)(2,1)}), bf16[4,1,8,4096]{3,2,1,0:T(8,128)(2,1)S(1)}, u32[]{:S(2)}, u32[]{:S(2)}) %all-to-all-start.4) | async-done | bytes 262176 | tf_op jit(solution)/shard_map/all_to_all | solution.py:105
  122.1 4.6 %copy.57 = bf16[4,1,8,4096]{2,0,1,3:T(4,128)(2,1)} copy(bf16[4,1,8,4096]{3,2,1,0:T(8,128)(2,1)S(1)} %all-to-all-done.4) | data formatting | bytes 524288 | tf_op jit(solution)/shard_map/all_to_all | solution.py:105
  126.7 6.4 %reshape.370 = bf16[8,2,8192]{2,1,0:T(2,128)(2,1)} reshape(bf16[4096,1,4,8]{3,2,1,0:T(4,128)(2,1)} %bitcast.81) | data formatting | bytes 524288
  133.1 3.4 %all-to-all-start.5 = ((bf16[8,2,8192]{2,1,0:T(2,128)(2,1)}), bf16[8,2,8192]{2,1,0:T(2,128)(2,1)S(1)}, u32[]{:S(2)}, u32[]{:S(2)}) async-start(bf16[8,2,8192]{2,1,0:T(2,128)(2,1)} %reshape.370), calls=%async_computation.5 | async-start | bytes 524288 | tf_op jit(solution)/shard_map/all_to_all | solution.py:104
  136.5 0.7 fusion.19
  137.2 25.8 %psum.7 = f32[128,2]{1,0:T(8,128)S(1)} all-reduce(f32[128,2]{1,0:T(8,128)} %fusion.19), channel_id=1, replica_groups=mesh['grp'=4,'ep'=8] {'ep'}, use_global_device_ids=true, to_apply=%region_7.8 | all-reduce | flops 256 | bytes 2048 | tf_op jit(solution)/shard_map/psum | solution.py:122
  163.0 0.6 copy.62
  163.6 5.9 %reshape.371 = bf16[4096,1,4,8]{3,2,1,0:T(4,128)(2,1)} reshape(bf16[8,2,8192]{2,1,0:T(2,128)(2,1)S(1)} %all-to-all-done.5) | data formatting | bytes 524288
  169.5 6.9 %copy.58 = f32[4,1,8,8,512]{4,2,3,0,1:T(8,128)} copy(bf16[4,1,8,8,512]{2,0,4,3,1:T(4,128)(2,1)} %bitcast.82) | data formatting | bytes 786432 | tf_op jit(solution)/shard_map/convert_element_type | solution.py:111
  176.5 3.1 %gather_fusion.2 = f32[256,512]{1,0:T(8,128)} fusion(f32[256,512]{1,0:T(8,128)} %bitcast.79, s32[1024]{0:T(1024)S(1)} %pad_clamp_fusion), kind=kCustom, calls=%fused_computation.2 | custom fusion | bytes 1049600 | tf_op jit(solution)/shard_map/gather | solution.py:117
  179.5 2.1 %reshape.313 = f32[128,2,512]{2,1,0:T(2,128)} reshape(f32[256,512]{1,0:T(8,128)} %gather_fusion.2) | data formatting | bytes 1048576 | tf_op jit(solution)/shard_map/reshape | solution.py:118
  181.7 2.4 %multiply_reduce_fusion = bf16[128,512]{1,0:T(8,128)(2,1)} fusion(f32[128,2,512]{2,1,0:T(2,128)} %reshape.313, f32[128,2]{1,0:T(8,128)S(1)} %copy-done.5), kind=kLoop, calls=%fused_computation.23 | loop fusion | flops 196608 | bytes 656384 | tf_op jit(solution)/shard_map/reduce_sum | solution.py:119
  (28 shorter events, 0.2 us)
Async XLA Ops:
  0.6 74.4 %copy-start = (bf16[1,384,4096]{2,1,0:T(8,128)(2,1)S(1)}, bf16[1,384,4096]{2,1,0:T(8,128)(2,1)}, u32[]{:S(2)}) copy-start(bf16[1,384,4096]{2,1,0:T(8,128)(2,1)} %param.12) | copy-start | bytes 9437188
  0.6 6.2 %copy-start.1 = (bf16[128,512]{1,0:T(8,128)(2,1)S(1)}, bf16[128,512]{1,0:T(8,128)(2,1)}, u32[]{:S(2)}) copy-start(bf16[128,512]{1,0:T(8,128)(2,1)} %param.7) | copy-start | bytes 393220
  37.5 19.4 %all-to-all-start = ((bf16[4,8,8,512]{3,2,1,0:T(8,128)(2,1)}), bf16[4,8,8,512]{3,2,1,0:T(8,128)(2,1)}, u32[]{:S(2)}, u32[]{:S(2)}) async-start(bf16[4,8,8,512]{3,2,1,0:T(8,128)(2,1)} %get-tuple-element.13), calls=%async_computation | async-start | bytes 524288 | tf_op jit(solution)/shard_map/all_to_all | solution.py:80
  42.2 29.5 %collective-permute-start.1 = (bf16[4,1,8,4096]{3,2,0,1:T(8,128)(2,1)}, bf16[4,1,8,4096]{3,2,0,1:T(8,128)(2,1)}, u32[]{:S(2)}, u32[]{:S(2)}) collective-permute-start(bf16[4,1,8,4096]{3,2,0,1:T(8,128)(2,1)} %bitcast.38), channel_id=1, source_target_pairs={{0,16},{8,24},{16,0},{24,8},{1,17},{9,25},{17,1},{25,9},{2,18},{10... | collective-permute-start | bytes 786440 | tf_op jit(solution)/shard_map/ppermute | solution.py:12
  58.5 11.0 %all-to-all-start.1 = ((bf16[4,8,8,512]{3,2,0,1:T(8,128)(2,1)}), bf16[4,8,8,512]{3,2,0,1:T(8,128)(2,1)}, u32[]{:S(2)}, u32[]{:S(2)}) async-start(bf16[4,8,8,512]{3,2,0,1:T(8,128)(2,1)} %copy.49), calls=%async_computation.1 | async-start | bytes 524288 | tf_op jit(solution)/shard_map/all_to_all | solution.py:79
  70.5 12.6 %collective-permute-start = (bf16[4,1,8,4096]{3,2,0,1:T(8,128)(2,1)S(1)}, bf16[4,1,8,4096]{3,2,0,1:T(8,128)(2,1)S(1)}, u32[]{:S(2)}, u32[]{:S(2)}) collective-permute-start(bf16[4,1,8,4096]{3,2,0,1:T(8,128)(2,1)S(1)} %bitcast.93), channel_id=1, source_target_pairs={{0,16},{8,24},{16,0},{24,8},{1,17},{9,25},{17,1},{25,9},{2,18},{10... | collective-permute-start | bytes 786440 | tf_op jit(solution)/shard_map/ppermute | solution.py:12
  71.8 11.3 %copy-start.3 = (bf16[1,384,4096]{2,1,0:T(8,128)(2,1)S(1)}, bf16[1,384,4096]{2,1,0:T(8,128)(2,1)}, u32[]{:S(2)}) copy-start(bf16[1,384,4096]{2,1,0:T(8,128)(2,1)} %param.13) | copy-start | bytes 9437188
  75.0 9.1 %copy-start.2 = (bf16[1,384,4096]{2,1,0:T(8,128)(2,1)S(1)}, bf16[1,384,4096]{2,1,0:T(8,128)(2,1)}, u32[]{:S(2)}) copy-start(bf16[1,384,4096]{2,1,0:T(8,128)(2,1)} %param.11) | copy-start | bytes 9437188
  84.9 7.4 %copy-start.6 = (f32[128,2]{0,1:T(2,128)S(1)}, f32[128,2]{0,1:T(2,128)}, u32[]{:S(2)}) copy-start(f32[128,2]{0,1:T(2,128)} %param.10) | copy-start | bytes 3076
  85.6 0.8 copy-start.4
  87.1 18.0 %collective-permute-start.2 = (bf16[4,1,8,4096]{3,2,1,0:T(8,128)(2,1)}, bf16[4,1,8,4096]{3,2,1,0:T(8,128)(2,1)S(1)}, u32[]{:S(2)}, u32[]{:S(2)}) collective-permute-start(bf16[4,1,8,4096]{3,2,1,0:T(8,128)(2,1)} %slice_bitcast_fusion), channel_id=1, source_target_pairs={{0,16},{8,24},{16,0},{24,8},{1,17},{9,25},{17,1},{25,9},{2,18},{10... | collective-permute-start | bytes 786440 | tf_op jit(solution)/shard_map/ppermute | solution.py:12
  88.0 13.9 %all-to-all-start.7 = ((f32[4,1,8]{2,1,0:T(1,128)}), f32[4,1,8]{2,1,0:T(1,128)S(1)}, u32[]{:S(2)}, u32[]{:S(2)}) async-start(f32[4,1,8]{2,1,0:T(1,128)} %bitcast.25), calls=%async_computation.7 | async-start | bytes 4096 | tf_op jit(solution)/shard_map/all_to_all | solution.py:114
  101.8 8.6 %all-to-all-start.6 = ((f32[4,1,8]{2,1,0:T(1,128)}), f32[4,1,8]{2,1,0:T(1,128)S(1)}, u32[]{:S(2)}, u32[]{:S(2)}) async-start(f32[4,1,8]{2,1,0:T(1,128)} %bitcast.23), calls=%async_computation.6 | async-start | bytes 4096 | tf_op jit(solution)/shard_map/all_to_all | solution.py:113
  110.4 11.6 %all-to-all-start.4 = ((bf16[4,1,8,4096]{3,2,1,0:T(8,128)(2,1)}), bf16[4,1,8,4096]{3,2,1,0:T(8,128)(2,1)S(1)}, u32[]{:S(2)}, u32[]{:S(2)}) async-start(bf16[4,1,8,4096]{3,2,1,0:T(8,128)(2,1)} %fusion.13), calls=%async_computation.4 | async-start | bytes 524288 | tf_op jit(solution)/shard_map/all_to_all | solution.py:105
  133.1 30.5 %all-to-all-start.5 = ((bf16[8,2,8192]{2,1,0:T(2,128)(2,1)}), bf16[8,2,8192]{2,1,0:T(2,128)(2,1)S(1)}, u32[]{:S(2)}, u32[]{:S(2)}) async-start(bf16[8,2,8192]{2,1,0:T(2,128)(2,1)} %reshape.370), calls=%async_computation.5 | async-start | bytes 524288 | tf_op jit(solution)/shard_map/all_to_all | solution.py:104
  176.5 5.2 %copy-start.5 = (f32[128,2]{1,0:T(8,128)S(1)}, f32[128,2]{1,0:T(8,128)}, u32[]{:S(2)}) copy-start(f32[128,2]{1,0:T(8,128)} %copy.59) | copy-start | bytes 3076
where the time goes:
time: 185 us; the launch traced here: 184 us
  blocking collectives  51.2 us (28%)
  local copies, waits for them, and re-layouts  49.4 us (27%)
  waiting for transfers between devices  41.6 us (22%)
  starting transfers between devices  25.4 us (14%)
  matrix products  7.88 us (4%)
  other arithmetic  7.68 us (4%)
    psum x1, blocking collectives, on_device(): grad_gates = lax.psum(gate_part.reshape(group_tokens, TOP), 'ep')  25.8 us
    unnamed x21, local copies, waits for them, and re-layouts  15.6 us
    all_to_all x1, blocking collectives, on_device(): lax.all_to_all(send_in, 'grp', split_axis=0, concat_axis=0, tiled=True)  15 us
    all_to_all x1, waiting for transfers between devices, on_device(): lax.all_to_all(send_back, 'grp', split_axis=0, concat_axis=0, tiled=True)  11.7 us
    all_to_all x1, blocking collectives, on_device(): lax.all_to_all(lax.all_to_all(send_in, 'grp', split_axis=0, concat_axis=0...  10.5 us
    all_to_all x1, waiting for transfers between devices, on_device(): lax.all_to_all(other_inner, 'grp', split_axis=0, concat_axis=0, tiled=True)  8.18 us
    convert_element_type x1, local copies, waits for them, and re-layouts, on_device(): summed = arrived.astype(jnp.float32)  6.94 us
    all_to_all x1, waiting for transfers between devices, on_device(): lax.all_to_all(lax.all_to_all(send_back, 'grp', split_axis=0, concat_axis...  6.54 us
  transfers between devices with their start and end apart: 9, of which 6 were waited for; matrix products, arithmetic and copies ran while one was open for 9% of the time, Pallas kernels for 0%

commit v1 on v0

v1 whole, which is shorter than its diff:
```python
import jax
import jax.numpy as jnp
from jax import lax
from jax.sharding import PartitionSpec as P

TOP = 2
EXTRA = 128


def half_terms(rows_in, rows_back, gate_half, up_half, down_half):
    contract = (((1,), (1,)), ((), ()))
    gate_pre = lax.dot_general(rows_in, gate_half, contract, preferred_element_type=jnp.float32)
    up_pre = lax.dot_general(rows_in, up_half, contract, preferred_element_type=jnp.float32)
    back_proj = lax.dot_general(rows_back, down_half, contract, preferred_element_type=jnp.float32)
    sigmoid_gate = jax.nn.sigmoid(gate_pre)
    active = gate_pre * sigmoid_gate
    hidden = (active * up_pre).astype(jnp.bfloat16)
    hidden = lax.optimization_barrier(hidden)
    inner_sum = jnp.sum(hidden.astype(jnp.float32) * back_proj, axis=1)
    grad_gate_pre = (
        back_proj * up_pre * sigmoid_gate * (1.0 + gate_pre * (1.0 - sigmoid_gate))
    ).astype(jnp.bfloat16)
    grad_up_pre = (back_proj * active).astype(jnp.bfloat16)
    partial_value = jnp.dot(grad_gate_pre, gate_half, preferred_element_type=jnp.float32)
    partial_value = partial_value + jnp.dot(
        grad_up_pre, up_half, preferred_element_type=jnp.float32
    )
    return (inner_sum, partial_value.astype(jnp.bfloat16))


def split_float(value):
    first = value.astype(jnp.bfloat16)
    rest = value - first.astype(jnp.float32)
    second = rest.astype(jnp.bfloat16)
    third = (rest - second.astype(jnp.float32)).astype(jnp.bfloat16)
    return jnp.stack([first, second, third], axis=-1)


def slot_tables(routes, pair_count, rank_count, cap):
    flat_expert = routes.reshape(-1)
    route_total = flat_expert.shape[0]
    onehot = (flat_expert[:, None] == jnp.arange(pair_count, dtype=jnp.int32)[None, :]).astype(
        jnp.int32
    )
    running = jnp.cumsum(onehot, axis=0)
    slot_index = flat_expert * cap + jnp.sum((running - 1) * onehot, axis=1)
    slot_total = pair_count * cap
    source_token = (
        jnp.zeros((slot_total,), jnp.int32)
        .at[slot_index]
        .set(jnp.arange(route_total, dtype=jnp.int32) // TOP)
    )
    filled = jnp.zeros((slot_total,), jnp.bool_).at[slot_index].set(True)
    return slot_index, source_token, filled


def on_device(tokens, grad_out, routes, route_weights, gate_weight, up_weight, down_weight):
    group_count = lax.axis_size("grp")
    rank_count = lax.axis_size("ep")
    pair_count = group_count // 2
    both = ("grp", "ep")
    group_tokens, feat_width = tokens.shape
    full_width = feat_width * rank_count
    per_device = group_tokens // rank_count
    slots = 2 * ((per_device * TOP + 2 * pair_count - 1) // (2 * pair_count))
    cap = rank_count * slots
    dense = pair_count == TOP and cap == group_tokens

    def by_half(values):
        blocks = values.reshape(-1, pair_count, rank_count, slots, values.shape[-1])
        return jnp.broadcast_to(blocks, (2,) + blocks.shape[1:])

    paired = jnp.concatenate([tokens, grad_out], axis=1)
    if dense:
        packed = jnp.broadcast_to(paired[None], (pair_count,) + paired.shape)
    else:
        slot_index, source_token, filled = slot_tables(routes, pair_count, rank_count, cap)
        packed = jnp.where(filled[:, None], paired[source_token], jnp.zeros((), paired.dtype))
    send = by_half(packed).reshape(group_count * rank_count, slots, 2 * feat_width)
    held = lax.all_to_all(send, both, split_axis=0, concat_axis=0, tiled=True)
    held = held.reshape(group_count, rank_count, slots, 2, feat_width)
    held = held.transpose(3, 0, 2, 1, 4).reshape(2, group_count * slots, full_width)
    inner_sum, partial_value = half_terms(
        held[0], held[1], gate_weight[0], up_weight[0], down_weight[0]
    )
    back = partial_value.reshape(group_count, slots, rank_count, feat_width).transpose(0, 2, 1, 3)
    parts = split_float(inner_sum).reshape(group_count, 1, slots, 3)
    parts = jnp.pad(parts, ((0, 0), (0, 0), (0, 0), (0, EXTRA - 3)))
    parts = jnp.broadcast_to(parts, (group_count, rank_count, slots, EXTRA))
    back = jnp.concatenate([back, parts], axis=-1)
    back = back.reshape(group_count * rank_count, slots, feat_width + EXTRA)
    arrived = lax.all_to_all(back, both, split_axis=0, concat_axis=0, tiled=True)
    arrived = arrived.reshape(2, pair_count, cap, feat_width + EXTRA)
    value = arrived[..., :feat_width].astype(jnp.float32)
    inner = jnp.sum(arrived[..., feat_width : feat_width + 3].astype(jnp.float32), axis=(0, 3))
    pair_sum = value[0] + value[1]
    if dense:
        first_expert = routes[:, :1] == 0
        weight_first = jnp.where(first_expert, route_weights[:, :1], route_weights[:, 1:])
        weight_second = jnp.where(first_expert, route_weights[:, 1:], route_weights[:, :1])
        grad_tokens = pair_sum[0] * weight_first + pair_sum[1] * weight_second
        grad_gates = jnp.where(routes == 0, inner[0][:, None], inner[1][:, None])
    else:
        per_route = pair_sum.reshape(pair_count * cap, feat_width)[slot_index]
        weighted = per_route.reshape(group_tokens, TOP, feat_width) * route_weights[:, :, None]
        grad_tokens = jnp.sum(weighted, axis=1)
        grad_gates = inner.reshape(-1)[slot_index].reshape(group_tokens, TOP)
    return (grad_tokens.astype(jnp.bfloat16), grad_gates)


def solution(mesh):
    placed = (
        P("grp", "ep"),
        P("grp", "ep"),
        P("grp", None),
        P("grp", None),
        P("grp", None, None),
        P("grp", None, None),
        P("grp", None, None),
    )
    return jax.shard_map(
        on_device,
        mesh=mesh,
        in_specs=placed,
        out_specs=(P("grp", "ep"), P("grp", None)),
        check_vma=False,
    )
```

time: 185 us -> 76.8 us (0.42)
  local copies, waits for them, and re-layouts: 49.4 us -> 9.09 us
  waiting for transfers between devices: 41.6 us -> 17.9 us
  starting transfers between devices: 25.4 us -> 3.73 us
  blocking collectives: 51.2 us -> 33.4 us
  matrix products: 7.88 us -> 4.73 us
    psum x1 -> x0, blocking collectives: 25.8 us -> none  [on_device(): grad_gates = lax.psum(gate_part.reshape(group_tokens, TOP), 'ep')]
    all_to_all x6 -> x1, starting transfers between devices: 22.4 us -> 3.73 us  [on_device(): lax.all_to_all(back, both, split_axis=0, concat_axis=0, tiled=True)]
    all_to_all x6 -> x1, waiting for transfers between devices: 35.7 us -> 17.9 us  [on_device(): lax.all_to_all(back, both, split_axis=0, concat_axis=0, tiled=True)]
    unnamed x21 -> x13, local copies, waits for them, and re-layouts: 15.6 us -> 0.59 us
    all_to_all x9 -> x0, local copies, waits for them, and re-layouts: 10.5 us -> none  [the longest x1 4.59 us: on_device(): lax.all_to_all(pair_sum, 'grp', split_axis=0, concat_axis=0, tiled=True)]
    gather x5 -> x0, local copies, waits for them, and re-layouts: 9.6 us -> none  [the longest x2 3.97 us: pack_rows(): values[source_token]]
    all_to_all x2 -> x1, blocking collectives: 25.4 us -> 33.4 us  [on_device(): held = lax.all_to_all(send, both, split_axis=0, concat_axis=0, tiled=True)]
    convert_element_type x1 -> x0, local copies, waits for them, and re-layouts: 6.94 us -> none  [on_device(): summed = arrived.astype(jnp.float32)]
  transfers between devices with their start and end apart: 9 -> 1, of which waited for: 6 -> 1; matrix products, arithmetic and copies ran while one was open for 9% -> 0% of each run, Pallas kernels for 0% -> 0%
where the time goes in v1:
time: 76.8 us; the launch traced here: 76.4 us
  blocking collectives  33.4 us (43%)
  waiting for transfers between devices  17.9 us (23%)
  local copies, waits for them, and re-layouts  9.09 us (12%)
  other arithmetic  6.7 us (9%)
  matrix products  4.73 us (6%)
  starting transfers between devices  3.73 us (5%)
  between operations  0.84 us (1%)
    all_to_all x1, blocking collectives, on_device(): held = lax.all_to_all(send, both, split_axis=0, concat_axis=0, tiled=True)  33.4 us
    all_to_all x1, waiting for transfers between devices, on_device(): lax.all_to_all(back, both, split_axis=0, concat_axis=0, tiled=True)  17.9 us
    slice x2, local copies, waits for them, and re-layouts, on_device(): held[0]  4.04 us
    all_to_all x1, starting transfers between devices, on_device(): lax.all_to_all(back, both, split_axis=0, concat_axis=0, tiled=True)  3.73 us
    reshape x1, local copies, waits for them, and re-layouts, on_device(): held = held.reshape(group_count, rank_count, slots, 2, feat_width)  2.62 us
    concatenate x1, other arithmetic, on_device(): back = jnp.concatenate([back, parts], axis=-1)  1.94 us
  transfers between devices with their start and end apart: 1, of which 1 were waited for; matrix products, arithmetic and copies ran while one was open for 0% of the time, Pallas kernels for 0%

profile of v1, /device:TPU:0, one launch (start us, length us, event | category | flops | bytes accessed | tf_op | source)
XLA Modules:
  0.0 76.4 jit_solution(14944692318211907408)
XLA Ops:
  0.6 0.0 copy-start
  0.6 1.1 %pad_maximum_fusion.1 = bf16[128,1024]{1,0:T(8,128)(2,1)S(1)} fusion(bf16[128,512]{1,0:T(8,128)(2,1)} %param.8, bf16[128,512]{1,0:T(8,128)(2,1)} %param.7), kind=kLoop, calls=%fused_computation.25 | loop fusion | flops 524288 | bytes 524288 | tf_op jit(solution)/shard_map/concatenate | solution.py:73
  1.8 0.1 broadcast_in_dim.39
  1.9 33.4 %all_to_all.10 = bf16[32,16,1024]{2,1,0:T(8,128)(2,1)} all-to-all(bf16[32,16,1024]{2,1,0:T(8,128)(2,1)S(1)} %bitcast.64), channel_id=1, replica_groups=mesh['grp'=4,'ep'=8] {'grp','ep'}, dimensions={0} | all-to-all | bytes 2097152 | tf_op jit(solution)/shard_map/all_to_all | solution.py:80
  35.4 2.6 %reshape.88 = bf16[4,8,16,2,512]{4,3,2,1,0:T(2,128)(2,1)} reshape(bf16[32,16,1024]{2,1,0:T(8,128)(2,1)} %all_to_all.10) | data formatting | bytes 2097152 | tf_op jit(solution)/shard_map/reshape | solution.py:81
  38.0 0.0 copy-start.1
  38.0 3.5 %fusion.28 = (bf16[1,4,16,8,512]{4,0,2,3,1:T(2,128)(2,1)S(1)}, bf16[1,4,16,8,512]{4,0,2,3,1:T(2,128)(2,1)S(1)}) fusion(bf16[2,4,16,8,512]{4,0,2,3,1:T(2,128)(2,1)} %bitcast.61), kind=kLoop, calls=%fused_computation.49 | loop fusion | bytes 2097152 | tf_op jit(solution)/shard_map/slice | solution.py:84
  41.5 0.6 copy.13
  42.0 0.2 copy.17
  42.2 0.0 copy-done.1
  42.2 1.1 %fusion.3 = f32[64,384]{1,0:T(8,128)S(1)} fusion(bf16[64,4096]{1,0:T(8,128)(2,1)S(1)} %bitcast.62, bf16[1,384,4096]{2,1,0:T(8,128)(2,1)S(1)} %copy-done.1), kind=kOutput, calls=%fused_computation.4 | convolution fusion | flops 201326592 | bytes 3768320 | tf_op jit(solution)/shard_map/dot_general | solution.py:12
  43.3 0.0 copy-done
  43.3 0.0 copy-start.2
  43.3 1.1 %multiply_convert_fusion = (bf16[64,384]{1,0:T(8,128)(2,1)S(1)}, f32[64,384]{1,0:T(8,128)S(1)}) fusion(f32[64,384]{1,0:T(8,128)S(1)} %fusion.3, bf16[64,4096]{1,0:T(8,128)(2,1)S(1)} %bitcast.63, bf16[1,384,4096]{2,1,0:T(8,128)(2,1)S(1)} %copy-done), kind=kOutput, calls=%fused_computation.31 | convolution fusion | flops 201474048 | bytes 3915776 | tf_op jit(solution)/shard_map/dot_general | solution.py:13
  44.4 0.6 copy.12
  45.0 0.2 copy.16
  45.2 0.0 copy-done.2
  45.2 1.2 %multiply_reduce_fusion = (f32[64]{0:T(128)S(1)}, f32[64,384]{1,0:T(8,128)S(1)}) fusion(bf16[64,384]{1,0:T(8,128)(2,1)S(1)} %get-tuple-element.11, bf16[64,4096]{1,0:T(8,128)(2,1)S(1)} %bitcast.71, bf16[1,384,4096]{2,1,0:T(8,128)(2,1)S(1)} %copy-done.2), kind=kOutput, calls=%fused_computation.30 | convolution fusion | flops 201400256 | bytes 3817728 | tf_op jit(solution)/shard_map/dot_general | solution.py:14
  46.4 0.7 fusion.1
  47.1 0.7 fusion
  47.8 0.0 copy-start.3
  47.8 0.0 copy-start.4
  47.8 0.2 copy.18
  48.0 1.0 %copy.20 = bf16[4,16,8,512]{3,1,2,0:T(8,128)(2,1)} copy(bf16[4,16,8,512]{3,2,1,0:T(8,128)(2,1)S(1)} %bitcast.70) | data formatting | bytes 1048576 | tf_op jit(solution)/shard_map/reshape | solution.py:86
  49.0 0.1 reduce_sum.21
  49.1 0.1 copy.15
  49.2 1.9 %pad_maximum_fusion = bf16[4,8,16,640]{3,2,1,0:T(8,128)(2,1)} fusion(bf16[4,8,16,128]{3,2,1,0:T(8,128)(2,1)S(1)} %broadcast_in_dim.41, bf16[4,8,16,512]{3,2,1,0:T(8,128)(2,1)} %bitcast.69), kind=kLoop, calls=%fused_computation.11 | loop fusion | flops 1310720 | bytes 1310720 | tf_op jit(solution)/shard_map/concatenate | solution.py:90
  51.2 3.7 %all-to-all-start.1 = ((bf16[32,16,640]{2,1,0:T(8,128)(2,1)}), bf16[32,16,640]{2,1,0:T(8,128)(2,1)}, u32[]{:S(2)}, u32[]{:S(2)}) async-start(bf16[32,16,640]{2,1,0:T(8,128)(2,1)} %bitcast.65), calls=%async_computation.1 | async-start | bytes 1310720 | tf_op jit(solution)/shard_map/all_to_all | solution.py:92
  54.9 0.0 copy-done.3
  54.9 0.0 copy-done.4
  54.9 17.9 %all-to-all-done.1 = bf16[32,16,640]{2,1,0:T(8,128)(2,1)} async-done(((bf16[32,16,640]{2,1,0:T(8,128)(2,1)}), bf16[32,16,640]{2,1,0:T(8,128)(2,1)}, u32[]{:S(2)}, u32[]{:S(2)}) %all-to-all-start.1) | async-done | bytes 655392 | tf_op jit(solution)/shard_map/all_to_all | solution.py:92
  72.8 1.0 %convert_reduce_fusion = f32[2,128]{1,0:T(2,128)S(1)} fusion(bf16[2,2,128,640]{3,2,1,0:T(8,128)(2,1)} %bitcast.9), kind=kLoop, calls=%fused_computation.26 | loop fusion | flops 2816 | bytes 4096 | tf_op jit(solution)/shard_map/reduce_sum | solution.py:95
  73.8 1.2 %slice_convert_fusion = f32[2,2,128,512]{3,2,1,0:T(8,128)S(1)} fusion(bf16[2,2,128,640]{3,2,1,0:T(8,128)(2,1)} %bitcast.9), kind=kLoop, calls=%fused_computation.13 | loop fusion | flops 262144 | bytes 1572864 | tf_op jit(solution)/shard_map/convert_element_type | solution.py:94
  75.0 0.1 slice_add_fusion
  75.1 0.6 compare_select_fusion
  75.7 0.8 fusion.12
  (5 shorter events, 0.1 us)
Async XLA Ops:
  0.6 42.7 %copy-start = (bf16[1,384,4096]{2,1,0:T(8,128)(2,1)S(1)}, bf16[1,384,4096]{2,1,0:T(8,128)(2,1)}, u32[]{:S(2)}) copy-start(bf16[1,384,4096]{2,1,0:T(8,128)(2,1)} %param.12) | copy-start | bytes 9437188
  38.0 4.2 %copy-start.1 = (bf16[1,384,4096]{2,1,0:T(8,128)(2,1)S(1)}, bf16[1,384,4096]{2,1,0:T(8,128)(2,1)}, u32[]{:S(2)}) copy-start(bf16[1,384,4096]{2,1,0:T(8,128)(2,1)} %param.11) | copy-start | bytes 9437188
  43.3 1.9 %copy-start.2 = (bf16[1,384,4096]{2,1,0:T(8,128)(2,1)S(1)}, bf16[1,384,4096]{2,1,0:T(8,128)(2,1)}, u32[]{:S(2)}) copy-start(bf16[1,384,4096]{2,1,0:T(8,128)(2,1)} %param.13) | copy-start | bytes 9437188
  47.8 7.1 %copy-start.3 = (s32[128,2]{0,1:T(2,128)S(1)}, s32[128,2]{0,1:T(2,128)}, u32[]{:S(2)}) copy-start(s32[128,2]{0,1:T(2,128)} %param.9) | copy-start | bytes 3076
  47.8 7.1 %copy-start.4 = (f32[128,2]{0,1:T(2,128)S(1)}, f32[128,2]{0,1:T(2,128)}, u32[]{:S(2)}) copy-start(f32[128,2]{0,1:T(2,128)} %param.10) | copy-start | bytes 3076
  51.2 21.6 %all-to-all-start.1 = ((bf16[32,16,640]{2,1,0:T(8,128)(2,1)}), bf16[32,16,640]{2,1,0:T(8,128)(2,1)}, u32[]{:S(2)}, u32[]{:S(2)}) async-start(bf16[32,16,640]{2,1,0:T(8,128)(2,1)} %bitcast.65), calls=%async_computation.1 | async-start | bytes 1310720 | tf_op jit(solution)/shard_map/all_to_all | solution.py:92

commit v2 on v1

v2 whole, which is shorter than its diff:
```python
import jax
import jax.numpy as jnp
from jax import lax
from jax.experimental import pallas as pl
from jax.experimental.pallas import tpu as pltpu
from jax.sharding import PartitionSpec as P

TOP = 2
LANES = 128
PARTS = 3
VMEM_BYTES = 40 * 1024 * 1024


def gradients(gate_pre, up_pre, back_proj):
    sigmoid_gate = jax.nn.sigmoid(gate_pre)
    active = gate_pre * sigmoid_gate
    hidden = (active * up_pre).astype(jnp.bfloat16)
    product = hidden.astype(jnp.float32) * back_proj
    grad_gate_pre = back_proj * up_pre * sigmoid_gate * (1.0 + gate_pre * (1.0 - sigmoid_gate))
    grad_up_pre = back_proj * active
    return product, grad_gate_pre.astype(jnp.bfloat16), grad_up_pre.astype(jnp.bfloat16)


def times_rows(rows, weight):
    contract = (((1,), (1,)), ((), ()))
    return lax.dot_general(rows, weight, contract, preferred_element_type=jnp.float32)


def times_units(grads, weight):
    return jnp.dot(grads, weight, preferred_element_type=jnp.float32)


def split_float(value):
    first = value.astype(jnp.bfloat16).astype(jnp.float32)
    second = (value - first).astype(jnp.bfloat16).astype(jnp.float32)
    third = (value - first - second).astype(jnp.bfloat16).astype(jnp.float32)
    return first, second, third


def repeat_lanes(row, start, count):
    lane = lax.broadcasted_iota(jnp.int32, row.shape, 1)
    row = jnp.where((lane >= start) & (lane < start + count), row, 0.0)
    row = pltpu.roll(row, (LANES - start) % LANES, 1)
    while count < LANES:
        row = row + pltpu.roll(row, count, 1)
        count *= 2
    return row


def half_kernel(rows_ref, gate_ref, up_hbm, down_hbm, out_ref, up_ref, down_ref, arrived):
    group_count, rank_count, slots, width = rows_ref.shape
    width = width // 2
    total = group_count * slots
    copies = (
        pltpu.make_async_copy(up_hbm, up_ref, arrived.at[0]),
        pltpu.make_async_copy(down_hbm, down_ref, arrived.at[1]),
    )
    for copy in copies:
        copy.start()
    slices = [slice(rank * width, (rank + 1) * width) for rank in range(rank_count)]

    def project(lanes, weight_ref):
        value = 0.0
        for rank, columns in enumerate(slices):
            rows = rows_ref[:, rank, :, lanes].reshape(total, width)
            value = value + times_rows(rows, weight_ref[0, :, columns])
        return value

    gate_pre = project(slice(0, width), gate_ref)
    copies[0].wait()
    up_pre = project(slice(0, width), up_ref)
    copies[1].wait()
    back_proj = project(slice(width, 2 * width), down_ref)
    product, grad_gate_pre, grad_up_pre = gradients(gate_pre, up_pre, back_proj)

    folded = product[:, :LANES]
    for start in range(LANES, product.shape[1], LANES):
        folded = folded + product[:, start : start + LANES]
    folded = jnp.concatenate([folded, jnp.zeros((LANES - total, LANES), jnp.float32)], axis=0)
    inner_sum = jnp.sum(folded.T, axis=0, keepdims=True)
    extra = out_ref.shape[2] - slots * (width // LANES)
    line = lax.broadcasted_iota(jnp.int32, (extra, LANES), 0)
    for group in range(group_count):
        tail = jnp.zeros((extra, LANES), jnp.float32)
        for index, piece in enumerate(split_float(repeat_lanes(inner_sum, group * slots, slots))):
            tail = jnp.where(line == index, piece, tail)
        for rank in range(rank_count):
            out_ref[group, rank, slots * (width // LANES) :, :] = tail.astype(jnp.bfloat16)

    for rank, columns in enumerate(slices):
        partial = times_units(grad_gate_pre, gate_ref[0, :, columns])
        partial = partial + times_units(grad_up_pre, up_ref[0, :, columns])
        partial = partial.astype(jnp.bfloat16)
        for group in range(group_count):
            rows = slice(group * slots, (group + 1) * slots)
            for index in range(width // LANES):
                lanes = slice(index * LANES, (index + 1) * LANES)
                out_ref[group, rank, index * slots : (index + 1) * slots, :] = partial[rows, lanes]


def owner_kernel(parts_ref, routes_ref, weights_ref, grad_ref, gates_ref):
    _, rank_count, length, _ = parts_ref.shape
    total, width = grad_ref.shape
    slots = total // rank_count
    body = slots * (width // LANES)
    first = routes_ref[:1, :] == 0
    scale_first = jnp.where(first, weights_ref[:1, :], weights_ref[1:, :])
    scale_second = jnp.where(first, weights_ref[1:, :], weights_ref[:1, :])
    line = lax.broadcasted_iota(jnp.int32, (LANES, total), 0)
    turned = jnp.where(line == 0, scale_first, scale_second).T
    scales = (turned[:, :1], turned[:, 1:2])
    for rank in range(rank_count):
        rows = slice(rank * slots, (rank + 1) * slots)
        for index in range(width // LANES):
            place = slice(index * slots, (index + 1) * slots)
            value = 0.0
            for expert in range(TOP):
                pair = parts_ref[expert, rank, place, :].astype(jnp.float32)
                pair = pair + parts_ref[expert + TOP, rank, place, :].astype(jnp.float32)
                value = value + scales[expert][rows] * pair
            grad_ref[rows, index * LANES : (index + 1) * LANES] = value.astype(jnp.bfloat16)
    owner = lax.broadcasted_iota(jnp.int32, (length - body, LANES), 1) // slots
    inner = []
    for expert in range(TOP):
        value = jnp.zeros((length - body, LANES), jnp.float32)
        for rank in range(rank_count):
            pair = parts_ref[expert, rank, body:, :].astype(jnp.float32)
            pair = pair + parts_ref[expert + TOP, rank, body:, :].astype(jnp.float32)
            value = value + jnp.where(owner == rank, pair, 0.0)
        inner.append(jnp.sum(value, axis=0, keepdims=True))
    gates_ref[...] = jnp.where(routes_ref[...] == 0, inner[0], inner[1])


def every_expert(tokens, grad_out, routes, route_weights, gate_weight, up_weight, down_weight):
    group_count = lax.axis_size("grp")
    rank_count = lax.axis_size("ep")
    both = ("grp", "ep")
    group_tokens, width = tokens.shape
    slots = group_tokens // rank_count
    length = slots * (width // LANES) + 8
    whole = pl.BlockSpec(memory_space=pltpu.VMEM)
    there = pl.BlockSpec(memory_space=pltpu.HBM)
    params = pltpu.CompilerParams(vmem_limit_bytes=VMEM_BYTES)

    paired = jnp.concatenate([tokens, grad_out], axis=1)
    send = jnp.broadcast_to(paired[None], (group_count,) + paired.shape)
    send = send.reshape(group_count * rank_count, slots, 2 * width)
    held = lax.all_to_all(send, both, split_axis=0, concat_axis=0, tiled=True)
    back = pl.pallas_call(
        half_kernel,
        out_shape=jax.ShapeDtypeStruct((group_count, rank_count, length, LANES), jnp.bfloat16),
        in_specs=[whole, whole, there, there],
        out_specs=whole,
        scratch_shapes=[
            pltpu.VMEM(up_weight.shape, up_weight.dtype),
            pltpu.VMEM(down_weight.shape, down_weight.dtype),
            pltpu.SemaphoreType.DMA((2,)),
        ],
        compiler_params=params,
    )(
        held.reshape(group_count, rank_count, slots, 2 * width),
        gate_weight,
        up_weight,
        down_weight,
    )
    back = back.reshape(group_count * rank_count, length, LANES)
    arrived = lax.all_to_all(back, both, split_axis=0, concat_axis=0, tiled=True)
    grad_tokens, grad_gates = pl.pallas_call(
        owner_kernel,
        out_shape=(
            jax.ShapeDtypeStruct(tokens.shape, jnp.bfloat16),
            jax.ShapeDtypeStruct((TOP, group_tokens), jnp.float32),
        ),
        in_specs=[whole] * 3,
        out_specs=(whole, whole),
        compiler_params=params,
    )(arrived.reshape(group_count, rank_count, length, LANES), routes.T, route_weights.T)
    return grad_tokens, grad_gates.T


def slot_tables(routes, pair_count, cap):
    flat_expert = routes.reshape(-1)
    route_total = flat_expert.shape[0]
    onehot = (flat_expert[:, None] == jnp.arange(pair_count, dtype=jnp.int32)[None, :]).astype(
        jnp.int32
    )
    running = jnp.cumsum(onehot, axis=0)
    slot_index = flat_expert * cap + jnp.sum((running - 1) * onehot, axis=1)
    slot_total = pair_count * cap
    source_token = (
        jnp.zeros((slot_total,), jnp.int32)
        .at[slot_index]
        .set(jnp.arange(route_total, dtype=jnp.int32) // TOP)
    )
    filled = jnp.zeros((slot_total,), jnp.bool_).at[slot_index].set(True)
    return slot_index, source_token, filled


def by_slots(tokens, grad_out, routes, route_weights, gate_weight, up_weight, down_weight):
    group_count = lax.axis_size("grp")
    rank_count = lax.axis_size("ep")
    pair_count = group_count // 2
    both = ("grp", "ep")
    group_tokens, width = tokens.shape
    per_device = group_tokens // rank_count
    slots = 2 * ((per_device * TOP + 2 * pair_count - 1) // (2 * pair_count))
    cap = rank_count * slots
    extra = LANES
    slot_index, source_token, filled = slot_tables(routes, pair_count, cap)

    paired = jnp.concatenate([tokens, grad_out], axis=1)
    packed = jnp.where(filled[:, None], paired[source_token], jnp.zeros((), paired.dtype))
    send = packed.reshape(1, pair_count, rank_count, slots, 2 * width)
    send = jnp.broadcast_to(send, (2,) + send.shape[1:])
    send = send.reshape(group_count * rank_count, slots, 2 * width)
    held = lax.all_to_all(send, both, split_axis=0, concat_axis=0, tiled=True)
    held = held.reshape(group_count, rank_count, slots, 2, width)
    held = held.transpose(3, 0, 2, 1, 4).reshape(2, group_count * slots, rank_count * width)
    gate_pre = times_rows(held[0], gate_weight[0])
    up_pre = times_rows(held[0], up_weight[0])
    back_proj = times_rows(held[1], down_weight[0])
    product, grad_gate_pre, grad_up_pre = gradients(gate_pre, up_pre, back_proj)
    inner_sum = jnp.sum(product, axis=1, keepdims=True)
    partial = times_units(grad_gate_pre, gate_weight[0]) + times_units(grad_up_pre, up_weight[0])
    back = partial.astype(jnp.bfloat16).reshape(group_count, slots, rank_count, width)
    back = back.transpose(0, 2, 1, 3)
    parts = jnp.concatenate(split_float(inner_sum), axis=1).astype(jnp.bfloat16)
    parts = jnp.pad(parts, ((0, 0), (0, extra - PARTS))).reshape(group_count, 1, slots, extra)
    parts = jnp.broadcast_to(parts, (group_count, rank_count, slots, extra))
    back = jnp.concatenate([back, parts], axis=-1)
    back = back.reshape(group_count * rank_count, slots, width + extra)
    arrived = lax.all_to_all(back, both, split_axis=0, concat_axis=0, tiled=True)
    arrived = arrived.reshape(2, pair_count * cap, width + extra).astype(jnp.float32)
    per_route = (arrived[0] + arrived[1])[slot_index].reshape(group_tokens, TOP, width + extra)
    grad_tokens = jnp.sum(per_route[..., :width] * route_weights[:, :, None], axis=1)
    grad_gates = jnp.sum(per_route[..., width : width + PARTS], axis=2)
    return (grad_tokens.astype(jnp.bfloat16), grad_gates)


def on_device(*args):
    pair_count = lax.axis_size("grp") // 2
    return every_expert(*args) if pair_count == TOP else by_slots(*args)


def solution(mesh):
    placed = (
        P("grp", "ep"),
        P("grp", "ep"),
        P("grp", None),
        P("grp", None),
        P("grp", None, None),
        P("grp", None, None),
        P("grp", None, None),
    )
    return jax.shard_map(
        on_device,
        mesh=mesh,
        in_specs=placed,
        out_specs=(P("grp", "ep"), P("grp", None)),
        check_vma=False,
    )
```

time: 76.8 us -> 66.8 us (0.87)
  blocking collectives: 33.4 us -> 53.5 us
  waiting for transfers between devices: 17.9 us -> 0 us
  Pallas kernels: 0 us -> 7.4 us
  other arithmetic: 6.7 us -> 1.14 us
  local copies, waits for them, and re-layouts: 9.09 us -> 3.91 us
  matrix products: 4.73 us -> 0 us
  starting transfers between devices: 3.73 us -> 0 us
    all_to_all x1 -> x2, blocking collectives: 33.4 us -> 53.5 us  [the longest x1 33.3 us: every_expert(): held = lax.all_to_all(send, both, split_axis=0, concat_axis=0, tiled=True)]
    all_to_all x1 -> x0, waiting for transfers between devices: 17.9 us -> none  [on_device(): lax.all_to_all(back, both, split_axis=0, concat_axis=0, tiled=True)]
    pallas_call x0 -> x2, Pallas kernels: none -> 7.4 us  [the longest x1 6.53 us: every_expert(): pl.pallas_call(half_kernel, out_shape=jax.ShapeDtypeStruct((group_count,...]
    dot_general x5 -> x0, matrix products: 4.73 us -> none  [the longest x1 1.17 us: half_terms(): lax.dot_general(rows_back, down_half, contract, preferred_element_type=jn...]
    slice x3 -> x0, local copies, waits for them, and re-layouts: 4.6 us -> none  [the longest x2 4.04 us: on_device(): held[0]]
    all_to_all x1 -> x0, starting transfers between devices: 3.73 us -> none  [on_device(): lax.all_to_all(back, both, split_axis=0, concat_axis=0, tiled=True)]
    reshape x2 -> x0, local copies, waits for them, and re-layouts: 3.58 us -> none  [the longest x1 2.62 us: on_device(): held = held.reshape(group_count, rank_count, slots, 2, feat_width)]
    unnamed x13 -> x10, local copies, waits for them, and re-layouts: 0.59 us -> 3.79 us
  transfers between devices with their start and end apart: 1 -> 0, of which waited for: 1 -> 0; matrix products, arithmetic and copies ran while one was open for 0% -> 0% of each run, Pallas kernels for 0% -> 0%
where the time goes in v2:
time: 66.8 us; the launch traced here: 66.6 us
  blocking collectives  53.5 us (80%)
  Pallas kernels  7.4 us (11%)
  local copies, waits for them, and re-layouts  3.91 us (6%)
  other arithmetic  1.14 us (2%)
  between operations  0.67 us (1%)
    all_to_all x1, blocking collectives, every_expert(): held = lax.all_to_all(send, both, split_axis=0, concat_axis=0, tiled=True)  33.3 us
    all_to_all x1, blocking collectives, every_expert(): lax.all_to_all(back, both, split_axis=0, concat_axis=0, tiled=True)  20.2 us
    pallas_call x1, Pallas kernels, every_expert(): pl.pallas_call(half_kernel, out_shape=jax.ShapeDtypeStruct((group_count,...  6.53 us
    unnamed x10, local copies, waits for them, and re-layouts  3.79 us

profile of v2, /device:TPU:0, one launch (start us, length us, event | category | flops | bytes accessed | tf_op | source)
XLA Modules:
  0.0 66.6 jit_solution(15847237430616006290)
XLA Ops:
  0.6 0.0 copy-start
  0.6 1.1 %pad_maximum_fusion = bf16[128,1024]{1,0:T(8,128)(2,1)S(1)} fusion(bf16[128,512]{1,0:T(8,128)(2,1)} %param.8, bf16[128,512]{1,0:T(8,128)(2,1)} %param.7), kind=kLoop, calls=%fused_computation | loop fusion | flops 524288 | bytes 524288 | tf_op jit(solution)/shard_map/concatenate | solution.py:145
  1.8 0.1 broadcast_in_dim.2
  1.9 33.3 %all_to_all.10 = bf16[32,16,1024]{2,1,0:T(8,128)(2,1)S(1)} all-to-all(bf16[32,16,1024]{2,1,0:T(8,128)(2,1)S(1)} %bitcast.12), channel_id=1, replica_groups=mesh['grp'=4,'ep'=8] {'grp','ep'}, dimensions={0} | all-to-all | bytes 2097152 | tf_op jit(solution)/shard_map/all_to_all | solution.py:148
  35.3 0.0 copy-done
  35.3 0.0 copy-start.1
  35.3 1.9 %copy-done.1 = bf16[1,384,4096]{2,1,0:T(8,128)(2,1)S(1)} copy-done((bf16[1,384,4096]{2,1,0:T(8,128)(2,1)S(1)}, bf16[1,384,4096]{2,1,0:T(8,128)(2,1)}, u32[]{:S(2)}) %copy-start.1) | copy-done | bytes 3145752
  37.1 0.0 copy-start.2
  37.1 1.9 %copy-done.2 = bf16[1,384,4096]{2,1,0:T(8,128)(2,1)S(1)} copy-done((bf16[1,384,4096]{2,1,0:T(8,128)(2,1)S(1)}, bf16[1,384,4096]{2,1,0:T(8,128)(2,1)}, u32[]{:S(2)}) %copy-start.2) | copy-done | bytes 3145752
  39.0 0.0 copy-start.3
  39.0 0.0 copy-start.4
  39.0 6.5 %shard_map.86 = bf16[4,8,72,128]{3,2,1,0:T(8,128)(2,1)S(1)} custom-call(bf16[4,8,16,1024]{3,2,1,0:T(8,128)(2,1)S(1)} %bitcast.7, bf16[1,384,4096]{2,1,0:T(8,128)(2,1)S(1)} %copy-done, bf16[1,384,4096]{2,1,0:T(8,128)(2,1)S(1)} %copy-done.1, bf16[1,384,4096]{2,1,0:T(8,128)(2,1)S(1)} %copy-done.2), custom_call_target="tpu_custom_call" | custom-call | tf_op jit(solution)/shard_map/pallas_call | solution.py:149
  45.6 20.2 %all_to_all.11 = bf16[32,72,128]{2,1,0:T(8,128)(2,1)S(1)} all-to-all(bf16[32,72,128]{2,1,0:T(8,128)(2,1)S(1)} %bitcast.9), channel_id=1, replica_groups=mesh['grp'=4,'ep'=8] {'grp','ep'}, dimensions={0} | all-to-all | bytes 1179648 | tf_op jit(solution)/shard_map/all_to_all | solution.py:167
  65.7 0.0 copy-done.3
  65.7 0.0 copy-done.4
  65.7 0.9 %shard_map.87 = (bf16[128,512]{1,0:T(8,128)(2,1)}, f32[2,128]{1,0:T(2,128)}) custom-call(bf16[4,8,72,128]{3,2,1,0:T(8,128)(2,1)S(1)} %bitcast.8, s32[2,128]{1,0:T(2,128)S(1)} %bitcast.10, f32[2,128]{1,0:T(2,128)S(1)} %bitcast.11), custom_call_target="tpu_custom_call" | custom-call | tf_op jit(solution)/shard_map/pallas_call | solution.py:168
Async XLA Ops:
  0.6 34.6 %copy-start = (bf16[1,384,4096]{2,1,0:T(8,128)(2,1)S(1)}, bf16[1,384,4096]{2,1,0:T(8,128)(2,1)}, u32[]{:S(2)}) copy-start(bf16[1,384,4096]{2,1,0:T(8,128)(2,1)} %gate_ref.1) | copy-start | bytes 9437188
  35.3 1.9 %copy-start.1 = (bf16[1,384,4096]{2,1,0:T(8,128)(2,1)S(1)}, bf16[1,384,4096]{2,1,0:T(8,128)(2,1)}, u32[]{:S(2)}) copy-start(bf16[1,384,4096]{2,1,0:T(8,128)(2,1)} %up_hbm.1) | copy-start | bytes 9437188
  37.1 1.9 %copy-start.2 = (bf16[1,384,4096]{2,1,0:T(8,128)(2,1)S(1)}, bf16[1,384,4096]{2,1,0:T(8,128)(2,1)}, u32[]{:S(2)}) copy-start(bf16[1,384,4096]{2,1,0:T(8,128)(2,1)} %down_hbm.1) | copy-start | bytes 9437188
  39.0 26.7 %copy-start.3 = (s32[128,2]{0,1:T(2,128)S(1)}, s32[128,2]{0,1:T(2,128)}, u32[]{:S(2)}) copy-start(s32[128,2]{0,1:T(2,128)} %param.9) | copy-start | bytes 3076
  39.0 26.7 %copy-start.4 = (f32[128,2]{0,1:T(2,128)S(1)}, f32[128,2]{0,1:T(2,128)}, u32[]{:S(2)}) copy-start(f32[128,2]{0,1:T(2,128)} %param.10) | copy-start | bytes 3076

commit v3 on v2

--- a/solution.py
+++ b/solution.py
@@ -7,7 +7,7 @@
 
 TOP = 2
 LANES = 128
-PARTS = 3
+PARTS = 2
 VMEM_BYTES = 40 * 1024 * 1024
 
 
@@ -33,8 +33,7 @@
 def split_float(value):
     first = value.astype(jnp.bfloat16).astype(jnp.float32)
     second = (value - first).astype(jnp.bfloat16).astype(jnp.float32)
-    third = (value - first - second).astype(jnp.bfloat16).astype(jnp.float32)
-    return first, second, third
+    return first, second
 
 
 def repeat_lanes(row, start, count):
@@ -47,62 +46,73 @@
     return row
 
 
-def half_kernel(rows_ref, gate_ref, up_hbm, down_hbm, out_ref, up_ref, down_ref, arrived):
+def pack_kernel(tokens_hbm, grad_hbm, up_hbm, out_ref, up_ref, tokens_ref, grad_ref, arrived):
+    width = tokens_ref.shape[1]
+    copies = [
+        pltpu.make_async_copy(tokens_hbm, tokens_ref, arrived.at[0]),
+        pltpu.make_async_copy(grad_hbm, grad_ref, arrived.at[1]),
+        pltpu.make_async_copy(up_hbm, up_ref, arrived.at[2]),
+    ]
+    for copy in copies:
+        copy.start()
+    copies[0].wait()
+    for group in range(out_ref.shape[0]):
+        out_ref[group, :, :width] = tokens_ref[...]
+    copies[1].wait()
+    for group in range(out_ref.shape[0]):
+        out_ref[group, :, width:] = grad_ref[...]
+    copies[2].wait()
+
+
+def half_kernel(rows_ref, gate_ref, up_ref, down_hbm, out_ref, down_ref, arrived):
     group_count, rank_count, slots, width = rows_ref.shape
     width = width // 2
     total = group_count * slots
-    copies = (
-        pltpu.make_async_copy(up_hbm, up_ref, arrived.at[0]),
-        pltpu.make_async_copy(down_hbm, down_ref, arrived.at[1]),
-    )
-    for copy in copies:
-        copy.start()
     slices = [slice(rank * width, (rank + 1) * width) for rank in range(rank_count)]
+    copy = pltpu.make_async_copy(down_hbm, down_ref, arrived.at[0])
+    copy.start()
 
     def project(lanes, weight_ref):
-        value = 0.0
-        for rank, columns in enumerate(slices):
-            rows = rows_ref[:, rank, :, lanes].reshape(total, width)
-            value = value + times_rows(rows, weight_ref[0, :, columns])
-        return value
-
-    gate_pre = project(slice(0, width), gate_ref)
-    copies[0].wait()
-    up_pre = project(slice(0, width), up_ref)
-    copies[1].wait()
-    back_proj = project(slice(width, 2 * width), down_ref)
-    product, grad_gate_pre, grad_up_pre = gradients(gate_pre, up_pre, back_proj)
+        rows = [rows_ref[:, rank, :, lanes].reshape(total, width) for rank in range(rank_count)]
+        return times_rows(jnp.concatenate(rows, axis=1), weight_ref[0])
+
+    first, second = slice(0, width), slice(width, 2 * width)
+    gate_pre = project(first, gate_ref)
+    up_pre = project(first, up_ref)
+    copy.wait()
+    back_proj = project(second, down_ref)
+    product, by_gate, by_up = gradients(gate_pre, up_pre, back_proj)
 
     folded = product[:, :LANES]
     for start in range(LANES, product.shape[1], LANES):
         folded = folded + product[:, start : start + LANES]
     folded = jnp.concatenate([folded, jnp.zeros((LANES - total, LANES), jnp.float32)], axis=0)
     inner_sum = jnp.sum(folded.T, axis=0, keepdims=True)
-    extra = out_ref.shape[2] - slots * (width // LANES)
-    line = lax.broadcasted_iota(jnp.int32, (extra, LANES), 0)
+    line = lax.broadcasted_iota(jnp.int32, (2, LANES), 0)
     for group in range(group_count):
-        tail = jnp.zeros((extra, LANES), jnp.float32)
+        tail = jnp.zeros((2, LANES), jnp.float32)
         for index, piece in enumerate(split_float(repeat_lanes(inner_sum, group * slots, slots))):
             tail = jnp.where(line == index, piece, tail)
         for rank in range(rank_count):
-            out_ref[group, rank, slots * (width // LANES) :, :] = tail.astype(jnp.bfloat16)
+            out_ref[group, rank, slots * (width // LANES) // 2] = tail.astype(jnp.bfloat16)
 
     for rank, columns in enumerate(slices):
-        partial = times_units(grad_gate_pre, gate_ref[0, :, columns])
-        partial = partial + times_units(grad_up_pre, up_ref[0, :, columns])
+        partial = times_units(by_gate, gate_ref[0, :, columns])
+        partial = partial + times_units(by_up, up_ref[0, :, columns])
         partial = partial.astype(jnp.bfloat16)
         for group in range(group_count):
             rows = slice(group * slots, (group + 1) * slots)
             for index in range(width // LANES):
                 lanes = slice(index * LANES, (index + 1) * LANES)
-                out_ref[group, rank, index * slots : (index + 1) * slots, :] = partial[rows, lanes]
+                place = slice(index * slots // 2, (index + 1) * slots // 2)
+                out_ref[group, rank, place] = partial[rows, lanes].reshape(slots // 2, 2, LANES)
 
 
 def owner_kernel(parts_ref, routes_ref, weights_ref, grad_ref, gates_ref):
-    _, rank_count, length, _ = parts_ref.shape
+    _, rank_count, length, _, _ = parts_ref.shape
     total, width = grad_ref.shape
     slots = total // rank_count
-    body = slots * (width // LANES)
+    body = slots * (width // LANES) // 2
     first = routes_ref[:1, :] == 0
     scale_first = jnp.where(first, weights_ref[:1, :], weights_ref[1:, :])
     scale_second = jnp.where(first, weights_ref[1:, :], weights_ref[:1, :])
@@ -112,20 +122,20 @@
     for rank in range(rank_count):
         rows = slice(rank * slots, (rank + 1) * slots)
         for index in range(width // LANES):
-            place = slice(index * slots, (index + 1) * slots)
+            place = slice(index * slots // 2, (index + 1) * slots // 2)
             value = 0.0
             for expert in range(TOP):
-                pair = parts_ref[expert, rank, place, :].astype(jnp.float32)
-                pair = pair + parts_ref[expert + TOP, rank, place, :].astype(jnp.float32)
+                pair = parts_ref[expert, rank, place].reshape(slots, LANES).astype(jnp.float32)
+                pair = pair + parts_ref[expert + TOP, rank, place].reshape(slots, LANES).astype(jnp.float32)
                 value = value + scales[expert][rows] * pair
             grad_ref[rows, index * LANES : (index + 1) * LANES] = value.astype(jnp.bfloat16)
-    owner = lax.broadcasted_iota(jnp.int32, (length - body, LANES), 1) // slots
+    owner = lax.broadcasted_iota(jnp.int32, (2, LANES), 1) // slots
     inner = []
     for expert in range(TOP):
-        value = jnp.zeros((length - body, LANES), jnp.float32)
+        value = jnp.zeros((2, LANES), jnp.float32)
         for rank in range(rank_count):
-            pair = parts_ref[expert, rank, body:, :].astype(jnp.float32)
-            pair = pair + parts_ref[expert + TOP, rank, body:, :].astype(jnp.float32)
+            pair = parts_ref[expert, rank, body].astype(jnp.float32)
+            pair = pair + parts_ref[expert + TOP, rank, body].astype(jnp.float32)
             value = value + jnp.where(owner == rank, pair, 0.0)
         inner.append(jnp.sum(value, axis=0, keepdims=True))
     gates_ref[...] = jnp.where(routes_ref[...] == 0, inner[0], inner[1])
@@ -137,33 +147,45 @@
     both = ("grp", "ep")
     group_tokens, width = tokens.shape
     slots = group_tokens // rank_count
-    length = slots * (width // LANES) + 8
+    length = slots * (width // LANES) // 2 + 1
     whole = pl.BlockSpec(memory_space=pltpu.VMEM)
     there = pl.BlockSpec(memory_space=pltpu.HBM)
     params = pltpu.CompilerParams(vmem_limit_bytes=VMEM_BYTES)
 
-    paired = jnp.concatenate([tokens, grad_out], axis=1)
-    send = jnp.broadcast_to(paired[None], (group_count,) + paired.shape)
+    send, up_weight = pl.pallas_call(
+        pack_kernel,
+        out_shape=[
+            jax.ShapeDtypeStruct((group_count, group_tokens, 2 * width), tokens.dtype),
+            jax.ShapeDtypeStruct(up_weight.shape, up_weight.dtype),
+        ],
+        in_specs=[there] * 3,
+        out_specs=[whole] * 2,
+        scratch_shapes=[
+            pltpu.VMEM(tokens.shape, tokens.dtype),
+            pltpu.VMEM(tokens.shape, tokens.dtype),
+            pltpu.SemaphoreType.DMA((3,)),
+        ],
+        compiler_params=params,
+    )(*[pltpu.with_memory_space_constraint(x, pltpu.HBM) for x in (tokens, grad_out, up_weight)])
     send = send.reshape(group_count * rank_count, slots, 2 * width)
     held = lax.all_to_all(send, both, split_axis=0, concat_axis=0, tiled=True)
     back = pl.pallas_call(
         half_kernel,
-        out_shape=jax.ShapeDtypeStruct((group_count, rank_count, length, LANES), jnp.bfloat16),
-        in_specs=[whole, whole, there, there],
+        out_shape=jax.ShapeDtypeStruct((group_count, rank_count, length, 2, LANES), jnp.bfloat16),
+        in_specs=[whole, whole, whole, there],
         out_specs=whole,
         scratch_shapes=[
-            pltpu.VMEM(up_weight.shape, up_weight.dtype),
             pltpu.VMEM(down_weight.shape, down_weight.dtype),
-            pltpu.SemaphoreType.DMA((2,)),
+            pltpu.SemaphoreType.DMA((1,)),
         ],
         compiler_params=params,
     )(
         held.reshape(group_count, rank_count, slots, 2 * width),
         gate_weight,
         up_weight,
-        down_weight,
-    )
-    back = back.reshape(group_count * rank_count, length, LANES)
+        pltpu.with_memory_space_constraint(down_weight, pltpu.HBM),
+    )
+    back = back.reshape(group_count * rank_count, length, 2, LANES)
     arrived = lax.all_to_all(back, both, split_axis=0, concat_axis=0, tiled=True)
     grad_tokens, grad_gates = pl.pallas_call(
         owner_kernel,
@@ -174,7 +196,7 @@
         in_specs=[whole] * 3,
         out_specs=(whole, whole),
         compiler_params=params,
-    )(arrived.reshape(group_count, rank_count, length, LANES), routes.T, route_weights.T)
+    )(arrived.reshape(group_count, rank_count, length, 2, LANES), routes.T, route_weights.T)
     return grad_tokens, grad_gates.T
 
 
@@ -238,8 +260,8 @@
 
 
 def on_device(*args):
-    pair_count = lax.axis_size("grp") // 2
-    return every_expert(*args) if pair_count == TOP else by_slots(*args)
+    everywhere = lax.axis_size("grp") // 2 == TOP and args[0].shape[0] == LANES
+    return every_expert(*args) if everywhere else by_slots(*args)
 
 
 def solution(mesh):

time: 66.8 us -> 61.6 us (0.922)
  local copies, waits for them, and re-layouts: 3.91 us -> 0.01 us
  other arithmetic: 1.14 us -> 0 us
  blocking collectives: 53.5 us -> 52.6 us
  Pallas kernels: 7.4 us -> 8.13 us
    unnamed x10 -> x6, local copies, waits for them, and re-layouts: 3.79 us -> 0.01 us
    pallas_call x0 -> x1, Pallas kernels: none -> 2.19 us  [every_expert(): pl.pallas_call(pack_kernel, out_shape=[jax.ShapeDtypeStruct((group_count,...]
    pallas_call x1, Pallas kernels: 6.53 us -> 4.89 us  [every_expert(): pl.pallas_call(half_kernel, out_shape=jax.ShapeDtypeStruct((group_count,...]
    concatenate x1 -> x0, other arithmetic: 1.14 us -> none  [every_expert(): paired = jnp.concatenate([tokens, grad_out], axis=1)]
    all_to_all x1, blocking collectives: 20.2 us -> 19.3 us  [every_expert(): lax.all_to_all(back, both, split_axis=0, concat_axis=0, tiled=True)]
where the time goes in v3:
time: 61.6 us; the launch traced here: 61.4 us
  blocking collectives  52.6 us (85%)
  Pallas kernels  8.13 us (13%)
  between operations  0.66 us (1%)
    all_to_all x1, blocking collectives, every_expert(): held = lax.all_to_all(send, both, split_axis=0, concat_axis=0, tiled=True)  33.3 us
    all_to_all x1, blocking collectives, every_expert(): lax.all_to_all(back, both, split_axis=0, concat_axis=0, tiled=True)  19.3 us
    pallas_call x1, Pallas kernels, every_expert(): pl.pallas_call(half_kernel, out_shape=jax.ShapeDtypeStruct((group_count,...  4.89 us
    pallas_call x1, Pallas kernels, every_expert(): pl.pallas_call(pack_kernel, out_shape=[jax.ShapeDtypeStruct((group_count,...  2.19 us

profile of v3, /device:TPU:0, one launch (start us, length us, event | category | flops | bytes accessed | tf_op | source)
XLA Modules:
  0.0 61.4 jit_solution(248643867238567404)
XLA Ops:
  0.6 0.0 copy-start
  0.6 2.2 %shard_map.86 = (bf16[4,128,1024]{2,1,0:T(8,128)(2,1)S(1)}, bf16[1,384,4096]{2,1,0:T(8,128)(2,1)S(1)}) custom-call(bf16[128,512]{1,0:T(8,128)(2,1)} %tokens_hbm.1, bf16[128,512]{1,0:T(8,128)(2,1)} %grad_hbm.1, bf16[1,384,4096]{2,1,0:T(8,128)(2,1)} %up_hbm.1), custom_call_target="tpu_custom_call" | custom-call | tf_op jit(solution)/shard_map/pallas_call | solution.py:155
  2.8 33.3 %all_to_all.10 = bf16[32,16,1024]{2,1,0:T(8,128)(2,1)S(1)} all-to-all(bf16[32,16,1024]{2,1,0:T(8,128)(2,1)S(1)} %bitcast.10), channel_id=1, replica_groups=mesh['grp'=4,'ep'=8] {'grp','ep'}, dimensions={0} | all-to-all | bytes 2097152 | tf_op jit(solution)/shard_map/all_to_all | solution.py:171
  36.2 0.0 copy-done
  36.2 0.0 copy-start.1
  36.2 0.0 copy-start.2
  36.2 4.9 %shard_map.87 = bf16[4,8,33,2,128]{4,3,2,1,0:T(2,128)(2,1)S(1)} custom-call(bf16[4,8,16,1024]{3,2,1,0:T(8,128)(2,1)S(1)} %bitcast.7, bf16[1,384,4096]{2,1,0:T(8,128)(2,1)S(1)} %copy-done, bf16[1,384,4096]{2,1,0:T(8,128)(2,1)S(1)} %get-tuple-element.7.up_ref, bf16[1,384,4096]{2,1,0:T(8,128)(2,1)} %down_hbm.1), custom_call_target="tpu_custom_call" | custom-call | tf_op jit(solution)/shard_map/pallas_call | solution.py:172
  41.1 19.3 %all_to_all.11 = bf16[32,33,2,128]{3,2,1,0:T(2,128)(2,1)S(1)} all-to-all(bf16[32,33,2,128]{3,2,1,0:T(2,128)(2,1)S(1)} %bitcast.9), channel_id=1, replica_groups=mesh['grp'=4,'ep'=8] {'grp','ep'}, dimensions={0} | all-to-all | bytes 1081344 | tf_op jit(solution)/shard_map/all_to_all | solution.py:189
  60.4 0.0 copy-done.1
  60.4 0.0 copy-done.2
  60.4 1.1 %shard_map.88 = (bf16[128,512]{1,0:T(8,128)(2,1)}, f32[2,128]{1,0:T(2,128)}) custom-call(bf16[4,8,33,2,128]{4,3,2,1,0:T(2,128)(2,1)S(1)} %bitcast.8, s32[2,128]{1,0:T(2,128)S(1)} %bitcast.11, f32[2,128]{1,0:T(2,128)S(1)} %bitcast.12), custom_call_target="tpu_custom_call" | custom-call | tf_op jit(solution)/shard_map/pallas_call | solution.py:190
Async XLA Ops:
  0.6 35.6 %copy-start = (bf16[1,384,4096]{2,1,0:T(8,128)(2,1)S(1)}, bf16[1,384,4096]{2,1,0:T(8,128)(2,1)}, u32[]{:S(2)}) copy-start(bf16[1,384,4096]{2,1,0:T(8,128)(2,1)} %gate_ref.1) | copy-start | bytes 9437188
  36.2 24.2 %copy-start.1 = (s32[128,2]{0,1:T(2,128)S(1)}, s32[128,2]{0,1:T(2,128)}, u32[]{:S(2)}) copy-start(s32[128,2]{0,1:T(2,128)} %param.9) | copy-start | bytes 3076
  36.2 24.2 %copy-start.2 = (f32[128,2]{0,1:T(2,128)S(1)}, f32[128,2]{0,1:T(2,128)}, u32[]{:S(2)}) copy-start(f32[128,2]{0,1:T(2,128)} %param.10) | copy-start | bytes 3076

commit v4 on v3

--- a/solution.py
+++ b/solution.py
@@ -8,6 +8,7 @@
 TOP = 2
 LANES = 128
 PARTS = 2
+TILE = 256
 VMEM_BYTES = 40 * 1024 * 1024
 
 
@@ -46,42 +47,37 @@
     return row
 
 
-def pack_kernel(tokens_hbm, grad_hbm, up_hbm, out_ref, up_ref, tokens_ref, grad_ref, arrived):
-    width = tokens_ref.shape[1]
-    copies = [
-        pltpu.make_async_copy(tokens_hbm, tokens_ref, arrived.at[0]),
-        pltpu.make_async_copy(grad_hbm, grad_ref, arrived.at[1]),
-        pltpu.make_async_copy(up_hbm, up_ref, arrived.at[2]),
-    ]
-    for copy in copies:
-        copy.start()
-    copies[0].wait()
-    for group in range(out_ref.shape[0]):
-        out_ref[group, :, :width] = tokens_ref[...]
-    copies[1].wait()
-    for group in range(out_ref.shape[0]):
-        out_ref[group, :, width:] = grad_ref[...]
-    copies[2].wait()
-
-
-def half_kernel(rows_ref, gate_ref, up_ref, down_hbm, out_ref, down_ref, arrived):
+def half_kernel(rows_ref, gate_ref, up_ref, down_ref, out_ref):
     group_count, rank_count, slots, width = rows_ref.shape
     width = width // 2
     total = group_count * slots
     slices = [slice(rank * width, (rank + 1) * width) for rank in range(rank_count)]
-    copy = pltpu.make_async_copy(down_hbm, down_ref, arrived.at[0])
-    copy.start()
-
-    def project(lanes, weight_ref):
-        rows = [rows_ref[:, rank, :, lanes].reshape(total, width) for rank in range(rank_count)]
-        return times_rows(jnp.concatenate(rows, axis=1), weight_ref[0])
+
+    units = gate_ref.shape[1]
+    cut = units // TILE * TILE
+    main, rest = slice(0, cut), slice(cut, units)
+
+    def project(lanes, *weights):
+        value = 0.0
+        for rank, columns in enumerate(slices):
+            rows = rows_ref[:, rank, :, lanes].reshape(total, width)
+            block = [ref[0, part, columns] for ref, part in weights]
+            block = block[0] if len(block) == 1 else jnp.concatenate(block, axis=0)
+            value = value + times_rows(rows, block)
+        return value
 
     first, second = slice(0, width), slice(width, 2 * width)
-    gate_pre = project(first, gate_ref)
-    up_pre = project(first, up_ref)
-    copy.wait()
-    back_proj = project(second, down_ref)
-    product, by_gate, by_up = gradients(gate_pre, up_pre, back_proj)
+    gate_main = project(first, (gate_ref, main))
+    up_main = project(first, (up_ref, main))
+    both_rest = project(first, (gate_ref, rest), (up_ref, rest))
+    back_main = project(second, (down_ref, main))
+    back_rest = project(second, (down_ref, rest))
+    product_main, by_gate_main, by_up_main = gradients(gate_main, up_main, back_main)
+    product_rest, by_gate_rest, by_up_rest = gradients(
+        both_rest[:, : units - cut], both_rest[:, units - cut :], back_rest
+    )
+    product = jnp.concatenate([product_main, product_rest], axis=1)
+    by_rest = jnp.concatenate([by_gate_rest, by_up_rest], axis=1)
 
     folded = product[:, :LANES]
     for start in range(LANES, product.shape[1], LANES):
@@ -96,20 +92,23 @@
         for rank in range(rank_count):
             out_ref[group, rank, slots * (width // LANES) // 2] = tail.astype(jnp.bfloat16)
 
+    flat_ref = out_ref.reshape(group_count, rank_count, 2 * out_ref.shape[2], LANES)
     for rank, columns in enumerate(slices):
-        partial = times_units(by_gate, gate_ref[0, :, columns])
-        partial = partial + times_units(by_up, up_ref[0, :, columns])
+        weight_rest = jnp.concatenate([gate_ref[0, rest, columns], up_ref[0, rest, columns]], axis=0)
+        partial = times_units(by_gate_main, gate_ref[0, main, columns])
+        partial = partial + times_units(by_up_main, up_ref[0, main, columns])
+        partial = partial + times_units(by_rest, weight_rest)
         partial = partial.astype(jnp.bfloat16)
         for group in range(group_count):
             rows = slice(group * slots, (group + 1) * slots)
             for index in range(width // LANES):
                 lanes = slice(index * LANES, (index + 1) * LANES)
-                place = slice(index * slots // 2, (index + 1) * slots // 2)
-                out_ref[group, rank, place] = partial[rows, lanes].reshape(slots // 2, 2, LANES)
+                flat_ref[group, rank, index * slots : (index + 1) * slots, :] = partial[rows, lanes]
 
 
 def owner_kernel(parts_ref, routes_ref, weights_ref, grad_ref, gates_ref):
     _, rank_count, length, _, _ = parts_ref.shape
+    flat_ref = parts_ref.reshape(parts_ref.shape[0], rank_count, 2 * length, LANES)
     total, width = grad_ref.shape
     slots = total // rank_count
     body = slots * (width // LANES) // 2
@@ -122,11 +121,11 @@
     for rank in range(rank_count):
         rows = slice(rank * slots, (rank + 1) * slots)
         for index in range(width // LANES):
-            place = slice(index * slots // 2, (index + 1) * slots // 2)
+            place = slice(index * slots, (index + 1) * slots)
             value = 0.0
             for expert in range(TOP):
-                pair = parts_ref[expert, rank, place].reshape(slots, LANES).astype(jnp.float32)
-                pair = pair + parts_ref[expert + TOP, rank, place].reshape(slots, LANES).astype(jnp.float32)
+                pair = flat_ref[expert, rank, place].astype(jnp.float32)
+                pair = pair + flat_ref[expert + TOP, rank, place].astype(jnp.float32)
                 value = value + scales[expert][rows] * pair
             grad_ref[rows, index * LANES : (index + 1) * LANES] = value.astype(jnp.bfloat16)
     owner = lax.broadcasted_iota(jnp.int32, (2, LANES), 1) // slots
@@ -149,41 +148,26 @@
     slots = group_tokens // rank_count
     length = slots * (width // LANES) // 2 + 1
     whole = pl.BlockSpec(memory_space=pltpu.VMEM)
-    there = pl.BlockSpec(memory_space=pltpu.HBM)
     params = pltpu.CompilerParams(vmem_limit_bytes=VMEM_BYTES)
 
-    send, up_weight = pl.pallas_call(
-        pack_kernel,
-        out_shape=[
-            jax.ShapeDtypeStruct((group_count, group_tokens, 2 * width), tokens.dtype),
-            jax.ShapeDtypeStruct(up_weight.shape, up_weight.dtype),
-        ],
-        in_specs=[there] * 3,
-        out_specs=[whole] * 2,
-        scratch_shapes=[
-            pltpu.VMEM(tokens.shape, tokens.dtype),
-            pltpu.VMEM(tokens.shape, tokens.dtype),
-            pltpu.SemaphoreType.DMA((3,)),
-        ],
-        compiler_params=params,
-    )(*[pltpu.with_memory_space_constraint(x, pltpu.HBM) for x in (tokens, grad_out, up_weight)])
+    paired = jnp.concatenate([tokens, grad_out], axis=1)
+    send = jnp.broadcast_to(paired[None], (group_count,) + paired.shape)
+    swap = [(source, source ^ 1) for source in range(rank_count)]
+    up_weight = lax.ppermute(up_weight, "ep", swap)
+    down_weight = lax.ppermute(down_weight, "ep", swap)
     send = send.reshape(group_count * rank_count, slots, 2 * width)
     held = lax.all_to_all(send, both, split_axis=0, concat_axis=0, tiled=True)
     back = pl.pallas_call(
         half_kernel,
         out_shape=jax.ShapeDtypeStruct((group_count, rank_count, length, 2, LANES), jnp.bfloat16),
-        in_specs=[whole, whole, whole, there],
+        in_specs=[whole] * 4,
         out_specs=whole,
-        scratch_shapes=[
-            pltpu.VMEM(down_weight.shape, down_weight.dtype),
-            pltpu.SemaphoreType.DMA((1,)),
-        ],
         compiler_params=params,
     )(
         held.reshape(group_count, rank_count, slots, 2 * width),
         gate_weight,
         up_weight,
-        pltpu.with_memory_space_constraint(down_weight, pltpu.HBM),
+        down_weight,
     )
     back = back.reshape(group_count * rank_count, length, 2, LANES)
     arrived = lax.all_to_all(back, both, split_axis=0, concat_axis=0, tiled=True)
@@ -261,6 +245,7 @@
 
 def on_device(*args):
     everywhere = lax.axis_size("grp") // 2 == TOP and args[0].shape[0] == LANES
+    everywhere = everywhere and lax.axis_size("ep") % 2 == 0
     return every_expert(*args) if everywhere else by_slots(*args)
 
 

time: 61.6 us -> 60.7 us (0.985)
  Pallas kernels: 8.13 us -> 5.28 us
  other arithmetic: 0 us -> 1.29 us
    pallas_call x1 -> x0, Pallas kernels: 2.19 us -> none  [every_expert(): pl.pallas_call(pack_kernel, out_shape=[jax.ShapeDtypeStruct((group_count,...]
    concatenate x0 -> x1, other arithmetic: none -> 1.29 us  [every_expert(): paired = jnp.concatenate([tokens, grad_out], axis=1)]
    pallas_call x1, Pallas kernels: 4.89 us -> 4.23 us  [every_expert(): pl.pallas_call(half_kernel, out_shape=jax.ShapeDtypeStruct((group_count,...]
  transfers between devices with their start and end apart: 0 -> 2, of which waited for: 0 -> 0; matrix products, arithmetic and copies ran while one was open for 0% -> 2% of each run, Pallas kernels for 0% -> 0%
where the time goes in v4:
time: 60.7 us; the launch traced here: 60.6 us
  blocking collectives  52.6 us (87%)
  Pallas kernels  5.28 us (9%)
  other arithmetic  1.29 us (2%)
  between operations  0.69 us (1%)
    all_to_all x1, blocking collectives, every_expert(): held = lax.all_to_all(send, both, split_axis=0, concat_axis=0, tiled=True)  33.3 us
    all_to_all x1, blocking collectives, every_expert(): lax.all_to_all(back, both, split_axis=0, concat_axis=0, tiled=True)  19.3 us
    pallas_call x1, Pallas kernels, every_expert(): pl.pallas_call(half_kernel, out_shape=jax.ShapeDtypeStruct((group_count,...  4.23 us
    concatenate x1, other arithmetic, every_expert(): paired = jnp.concatenate([tokens, grad_out], axis=1)  1.29 us
  transfers between devices with their start and end apart: 2, of which 0 were waited for; matrix products, arithmetic and copies ran while one was open for 2% of the time, Pallas kernels for 0%

profile of v4, /device:TPU:0, one launch (start us, length us, event | category | flops | bytes accessed | tf_op | source)
XLA Modules:
  0.0 60.6 jit_solution(16734931843446809038)
XLA Ops:
  0.6 0.0 copy-start
  0.6 0.5 collective-permute-start
  1.2 0.1 collective-permute-start.1
  1.2 1.3 %pad_maximum_fusion = bf16[128,1024]{1,0:T(8,128)(2,1)S(1)} fusion(bf16[128,512]{1,0:T(8,128)(2,1)} %param.8, bf16[128,512]{1,0:T(8,128)(2,1)} %param.7), kind=kLoop, calls=%fused_computation | loop fusion | flops 524288 | bytes 524288 | tf_op jit(solution)/shard_map/concatenate | solution.py:153
  2.5 0.1 broadcast_in_dim.2
  2.7 33.3 %all_to_all.10 = bf16[32,16,1024]{2,1,0:T(8,128)(2,1)S(1)} all-to-all(bf16[32,16,1024]{2,1,0:T(8,128)(2,1)S(1)} %bitcast.12), channel_id=1, replica_groups=mesh['grp'=4,'ep'=8] {'grp','ep'}, dimensions={0} | all-to-all | bytes 2097152 | tf_op jit(solution)/shard_map/all_to_all | solution.py:159
  36.0 0.0 collective-permute-done.up_ref
  36.0 0.0 collective-permute-done.1.down_ref
  36.0 0.0 copy-done
  36.0 0.0 copy-start.1
  36.0 0.0 copy-start.2
  36.0 4.2 %shard_map.86 = bf16[4,8,33,2,128]{4,3,2,1,0:T(2,128)(2,1)S(1)} custom-call(bf16[4,8,16,1024]{3,2,1,0:T(8,128)(2,1)S(1)} %bitcast.7, bf16[1,384,4096]{2,1,0:T(8,128)(2,1)S(1)} %copy-done, bf16[1,384,4096]{2,1,0:T(8,128)(2,1)S(1)} %collective-permute-done.up_ref, bf16[1,384,4096]{2,1,0:T(8,128)(2,1)S(1)} %collective-permute-done.1.down_ref), custom_call_target="tpu_custom_call" | custom-call | tf_op jit(solution)/shard_map/pallas_call | solution.py:160
  40.2 19.3 %all_to_all.11 = bf16[32,33,2,128]{3,2,1,0:T(2,128)(2,1)S(1)} all-to-all(bf16[32,33,2,128]{3,2,1,0:T(2,128)(2,1)S(1)} %bitcast.9), channel_id=1, replica_groups=mesh['grp'=4,'ep'=8] {'grp','ep'}, dimensions={0} | all-to-all | bytes 1081344 | tf_op jit(solution)/shard_map/all_to_all | solution.py:173
  59.5 0.0 copy-done.1
  59.5 0.0 copy-done.2
  59.5 1.1 %shard_map.87 = (bf16[128,512]{1,0:T(8,128)(2,1)}, f32[2,128]{1,0:T(2,128)}) custom-call(bf16[4,8,33,2,128]{4,3,2,1,0:T(2,128)(2,1)S(1)} %bitcast.8, s32[2,128]{1,0:T(2,128)S(1)} %bitcast.10, f32[2,128]{1,0:T(2,128)S(1)} %bitcast.11), custom_call_target="tpu_custom_call" | custom-call | tf_op jit(solution)/shard_map/pallas_call | solution.py:174
Async XLA Ops:
  0.6 35.3 %copy-start = (bf16[1,384,4096]{2,1,0:T(8,128)(2,1)S(1)}, bf16[1,384,4096]{2,1,0:T(8,128)(2,1)}, u32[]{:S(2)}) copy-start(bf16[1,384,4096]{2,1,0:T(8,128)(2,1)} %gate_ref.1) | copy-start | bytes 9437188
  0.6 35.3 %collective-permute-start = (bf16[1,384,4096]{2,1,0:T(8,128)(2,1)}, bf16[1,384,4096]{2,1,0:T(8,128)(2,1)S(1)}, u32[]{:S(2)}, u32[]{:S(2)}) collective-permute-start(bf16[1,384,4096]{2,1,0:T(8,128)(2,1)} %param.12), channel_id=1, source_target_pairs={{0,1},{1,0},{2,3},{3,2},{4,5},{5,4},{6,7},{7,6},{8,9},{9,8},{10,11... | collective-permute-start | bytes 9437192 | tf_op jit(solution)/shard_map/ppermute | solution.py:156
  1.2 34.8 %collective-permute-start.1 = (bf16[1,384,4096]{2,1,0:T(8,128)(2,1)}, bf16[1,384,4096]{2,1,0:T(8,128)(2,1)S(1)}, u32[]{:S(2)}, u32[]{:S(2)}) collective-permute-start(bf16[1,384,4096]{2,1,0:T(8,128)(2,1)} %param.13), channel_id=1, source_target_pairs={{0,1},{1,0},{2,3},{3,2},{4,5},{5,4},{6,7},{7,6},{8,9},{9,8},{10,11... | collective-permute-start | bytes 9437192 | tf_op jit(solution)/shard_map/ppermute | solution.py:157
  36.0 23.5 %copy-start.1 = (s32[128,2]{0,1:T(2,128)S(1)}, s32[128,2]{0,1:T(2,128)}, u32[]{:S(2)}) copy-start(s32[128,2]{0,1:T(2,128)} %param.9) | copy-start | bytes 3076
  36.0 23.5 %copy-start.2 = (f32[128,2]{0,1:T(2,128)S(1)}, f32[128,2]{0,1:T(2,128)}, u32[]{:S(2)}) copy-start(f32[128,2]{0,1:T(2,128)} %param.10) | copy-start | bytes 3076

commit v5 on v4

--- a/solution.py
+++ b/solution.py
@@ -48,7 +48,7 @@
 
 
 def half_kernel(rows_ref, gate_ref, up_ref, down_ref, out_ref):
-    group_count, rank_count, slots, width = rows_ref.shape
+    rank_count, group_count, slots, width = rows_ref.shape
     width = width // 2
     total = group_count * slots
     slices = [slice(rank * width, (rank + 1) * width) for rank in range(rank_count)]
@@ -60,7 +60,7 @@
     def project(lanes, *weights):
         value = 0.0
         for rank, columns in enumerate(slices):
-            rows = rows_ref[:, rank, :, lanes].reshape(total, width)
+            rows = rows_ref[rank, :, :, lanes].reshape(total, width)
             block = [ref[0, part, columns] for ref, part in weights]
             block = block[0] if len(block) == 1 else jnp.concatenate(block, axis=0)
             value = value + times_rows(rows, block)
@@ -90,9 +90,9 @@
         for index, piece in enumerate(split_float(repeat_lanes(inner_sum, group * slots, slots))):
             tail = jnp.where(line == index, piece, tail)
         for rank in range(rank_count):
-            out_ref[group, rank, slots * (width // LANES) // 2] = tail.astype(jnp.bfloat16)
-
-    flat_ref = out_ref.reshape(group_count, rank_count, 2 * out_ref.shape[2], LANES)
+            out_ref[rank, group, slots * (width // LANES) // 2] = tail.astype(jnp.bfloat16)
+
+    flat_ref = out_ref.reshape(rank_count, group_count, 2 * out_ref.shape[2], LANES)
     for rank, columns in enumerate(slices):
         weight_rest = jnp.concatenate([gate_ref[0, rest, columns], up_ref[0, rest, columns]], axis=0)
         partial = times_units(by_gate_main, gate_ref[0, main, columns])
@@ -103,12 +103,12 @@
             rows = slice(group * slots, (group + 1) * slots)
             for index in range(width // LANES):
                 lanes = slice(index * LANES, (index + 1) * LANES)
-                flat_ref[group, rank, index * slots : (index + 1) * slots, :] = partial[rows, lanes]
+                flat_ref[rank, group, index * slots : (index + 1) * slots, :] = partial[rows, lanes]
 
 
 def owner_kernel(parts_ref, routes_ref, weights_ref, grad_ref, gates_ref):
-    _, rank_count, length, _, _ = parts_ref.shape
-    flat_ref = parts_ref.reshape(parts_ref.shape[0], rank_count, 2 * length, LANES)
+    rank_count, _, length, _, _ = parts_ref.shape
+    flat_ref = parts_ref.reshape(rank_count, parts_ref.shape[1], 2 * length, LANES)
     total, width = grad_ref.shape
     slots = total // rank_count
     body = slots * (width // LANES) // 2
@@ -124,8 +124,8 @@
             place = slice(index * slots, (index + 1) * slots)
             value = 0.0
             for expert in range(TOP):
-                pair = flat_ref[expert, rank, place].astype(jnp.float32)
-                pair = pair + flat_ref[expert + TOP, rank, place].astype(jnp.float32)
+                pair = flat_ref[rank, expert, place].astype(jnp.float32)
+                pair = pair + flat_ref[rank, expert + TOP, place].astype(jnp.float32)
                 value = value + scales[expert][rows] * pair
             grad_ref[rows, index * LANES : (index + 1) * LANES] = value.astype(jnp.bfloat16)
     owner = lax.broadcasted_iota(jnp.int32, (2, LANES), 1) // slots
@@ -133,8 +133,8 @@
     for expert in range(TOP):
         value = jnp.zeros((2, LANES), jnp.float32)
         for rank in range(rank_count):
-            pair = parts_ref[expert, rank, body].astype(jnp.float32)
-            pair = pair + parts_ref[expert + TOP, rank, body].astype(jnp.float32)
+            pair = parts_ref[rank, expert, body].astype(jnp.float32)
+            pair = pair + parts_ref[rank, expert + TOP, body].astype(jnp.float32)
             value = value + jnp.where(owner == rank, pair, 0.0)
         inner.append(jnp.sum(value, axis=0, keepdims=True))
     gates_ref[...] = jnp.where(routes_ref[...] == 0, inner[0], inner[1])
@@ -143,28 +143,29 @@
 def every_expert(tokens, grad_out, routes, route_weights, gate_weight, up_weight, down_weight):
     group_count = lax.axis_size("grp")
     rank_count = lax.axis_size("ep")
-    both = ("grp", "ep")
+    both = ("ep", "grp")
     group_tokens, width = tokens.shape
     slots = group_tokens // rank_count
     length = slots * (width // LANES) // 2 + 1
     whole = pl.BlockSpec(memory_space=pltpu.VMEM)
     params = pltpu.CompilerParams(vmem_limit_bytes=VMEM_BYTES)
 
-    paired = jnp.concatenate([tokens, grad_out], axis=1)
-    send = jnp.broadcast_to(paired[None], (group_count,) + paired.shape)
+    paired = jnp.concatenate([tokens, grad_out], axis=1).reshape(rank_count, 1, slots, 2 * width)
+    send = jnp.broadcast_to(paired, (rank_count, group_count, slots, 2 * width))
     swap = [(source, source ^ 1) for source in range(rank_count)]
+    send, up_weight, down_weight = lax.optimization_barrier((send, up_weight, down_weight))
     up_weight = lax.ppermute(up_weight, "ep", swap)
     down_weight = lax.ppermute(down_weight, "ep", swap)
     send = send.reshape(group_count * rank_count, slots, 2 * width)
     held = lax.all_to_all(send, both, split_axis=0, concat_axis=0, tiled=True)
     back = pl.pallas_call(
         half_kernel,
-        out_shape=jax.ShapeDtypeStruct((group_count, rank_count, length, 2, LANES), jnp.bfloat16),
+        out_shape=jax.ShapeDtypeStruct((rank_count, group_count, length, 2, LANES), jnp.bfloat16),
         in_specs=[whole] * 4,
         out_specs=whole,
         compiler_params=params,
     )(
-        held.reshape(group_count, rank_count, slots, 2 * width),
+        held.reshape(rank_count, group_count, slots, 2 * width),
         gate_weight,
         up_weight,
         down_weight,
@@ -180,7 +181,7 @@
         in_specs=[whole] * 3,
         out_specs=(whole, whole),
         compiler_params=params,
-    )(arrived.reshape(group_count, rank_count, length, 2, LANES), routes.T, route_weights.T)
+    )(arrived.reshape(rank_count, group_count, length, 2, LANES), routes.T, route_weights.T)
     return grad_tokens, grad_gates.T
 
 

time: 60.7 us -> 59.8 us (0.985); the launches traced: 60.6 us -> 58.9 us
  blocking collectives: 52.6 us -> 51.1 us
    all_to_all x1, blocking collectives: 33.3 us -> 32.1 us  [every_expert(): held = lax.all_to_all(send, both, split_axis=0, concat_axis=0, tiled=True)]
  transfers between devices with their start and end apart: 2 -> 2, of which waited for: 0 -> 0; matrix products, arithmetic and copies ran while one was open for 2% -> 0% of each run, Pallas kernels for 0% -> 0%
where the time goes in v5:
time: 59.8 us; the launch traced here: 58.9 us
  blocking collectives  51.1 us (85%)
  Pallas kernels  5.27 us (9%)
  other arithmetic  1.14 us (2%)
  between operations  0.69 us (1%)
  starting transfers between devices  0.6 us (1%)
    all_to_all x1, blocking collectives, every_expert(): held = lax.all_to_all(send, both, split_axis=0, concat_axis=0, tiled=True)  32.1 us
    all_to_all x1, blocking collectives, every_expert(): lax.all_to_all(back, both, split_axis=0, concat_axis=0, tiled=True)  19 us
    pallas_call x1, Pallas kernels, every_expert(): pl.pallas_call(half_kernel, out_shape=jax.ShapeDtypeStruct((rank_count, g...  4.22 us
  transfers between devices with their start and end apart: 2, of which 0 were waited for; matrix products, arithmetic and copies ran while one was open for 0% of the time, Pallas kernels for 0%

profile of v5, /device:TPU:0, one launch (start us, length us, event | category | flops | bytes accessed | tf_op | source)
XLA Modules:
  0.0 58.9 jit_solution(17374811133171204936)
XLA Ops:
  0.6 0.0 copy-start
  0.6 1.1 %pad_maximum_fusion = bf16[128,1024]{1,0:T(8,128)(2,1)S(1)} fusion(bf16[128,512]{1,0:T(8,128)(2,1)} %param.8, bf16[128,512]{1,0:T(8,128)(2,1)} %param.7), kind=kLoop, calls=%fused_computation | loop fusion | flops 524288 | bytes 524288 | tf_op jit(solution)/shard_map/concatenate | solution.py:153
  1.8 0.1 broadcast_in_dim.8
  1.9 0.5 collective-permute-start
  2.4 0.1 collective-permute-start.1
  2.5 32.1 %all_to_all.10 = bf16[32,16,1024]{2,1,0:T(8,128)(2,1)S(1)} all-to-all(bf16[32,16,1024]{2,1,0:T(8,128)(2,1)S(1)} %bitcast.13), channel_id=1, replica_groups=mesh['grp'=4,'ep'=8] {'ep','grp'}, dimensions={0} | all-to-all | bytes 2097152 | tf_op jit(solution)/shard_map/all_to_all | solution.py:160
  34.6 0.0 collective-permute-done.up_ref
  34.6 0.0 collective-permute-done.1.down_ref
  34.6 0.0 copy-done
  34.7 0.0 copy-start.1
  34.7 0.0 copy-start.2
  34.7 4.2 %shard_map.86 = bf16[8,4,33,2,128]{4,3,2,1,0:T(2,128)(2,1)S(1)} custom-call(bf16[8,4,16,1024]{3,2,1,0:T(8,128)(2,1)S(1)} %bitcast.8, bf16[1,384,4096]{2,1,0:T(8,128)(2,1)S(1)} %copy-done, bf16[1,384,4096]{2,1,0:T(8,128)(2,1)S(1)} %collective-permute-done.up_ref, bf16[1,384,4096]{2,1,0:T(8,128)(2,1)S(1)} %collective-permute-done.1.down_ref), custom_call_target="tpu_custom_call" | custom-call | tf_op jit(solution)/shard_map/pallas_call | solution.py:161
  38.9 19.0 %all_to_all.11 = bf16[32,33,2,128]{3,2,1,0:T(2,128)(2,1)S(1)} all-to-all(bf16[32,33,2,128]{3,2,1,0:T(2,128)(2,1)S(1)} %bitcast.10), channel_id=1, replica_groups=mesh['grp'=4,'ep'=8] {'ep','grp'}, dimensions={0} | all-to-all | bytes 1081344 | tf_op jit(solution)/shard_map/all_to_all | solution.py:174
  57.9 0.0 copy-done.1
  57.9 0.0 copy-done.2
  57.9 1.1 %shard_map.87 = (bf16[128,512]{1,0:T(8,128)(2,1)}, f32[2,128]{1,0:T(2,128)}) custom-call(bf16[8,4,33,2,128]{4,3,2,1,0:T(2,128)(2,1)S(1)} %bitcast.9, s32[2,128]{1,0:T(2,128)S(1)} %bitcast.11, f32[2,128]{1,0:T(2,128)S(1)} %bitcast.12), custom_call_target="tpu_custom_call" | custom-call | tf_op jit(solution)/shard_map/pallas_call | solution.py:175
Async XLA Ops:
  0.6 34.0 %copy-start = (bf16[1,384,4096]{2,1,0:T(8,128)(2,1)S(1)}, bf16[1,384,4096]{2,1,0:T(8,128)(2,1)}, u32[]{:S(2)}) copy-start(bf16[1,384,4096]{2,1,0:T(8,128)(2,1)} %gate_ref.1) | copy-start | bytes 9437188
  1.9 32.7 %collective-permute-start = (bf16[1,384,4096]{2,1,0:T(8,128)(2,1)}, bf16[1,384,4096]{2,1,0:T(8,128)(2,1)S(1)}, u32[]{:S(2)}, u32[]{:S(2)}) collective-permute-start(bf16[1,384,4096]{2,1,0:T(8,128)(2,1)} %param.12), channel_id=1, source_target_pairs={{0,1},{1,0},{2,3},{3,2},{4,5},{5,4},{6,7},{7,6},{8,9},{9,8},{10,11... | collective-permute-start | bytes 9437192 | tf_op jit(solution)/shard_map/ppermute | solution.py:157
  2.4 32.2 %collective-permute-start.1 = (bf16[1,384,4096]{2,1,0:T(8,128)(2,1)}, bf16[1,384,4096]{2,1,0:T(8,128)(2,1)S(1)}, u32[]{:S(2)}, u32[]{:S(2)}) collective-permute-start(bf16[1,384,4096]{2,1,0:T(8,128)(2,1)} %param.13), channel_id=1, source_target_pairs={{0,1},{1,0},{2,3},{3,2},{4,5},{5,4},{6,7},{7,6},{8,9},{9,8},{10,11... | collective-permute-start | bytes 9437192 | tf_op jit(solution)/shard_map/ppermute | solution.py:158
  34.7 23.2 %copy-start.1 = (s32[128,2]{0,1:T(2,128)S(1)}, s32[128,2]{0,1:T(2,128)}, u32[]{:S(2)}) copy-start(s32[128,2]{0,1:T(2,128)} %param.9) | copy-start | bytes 3076
  34.7 23.2 %copy-start.2 = (f32[128,2]{0,1:T(2,128)S(1)}, f32[128,2]{0,1:T(2,128)}, u32[]{:S(2)}) copy-start(f32[128,2]{0,1:T(2,128)} %param.10) | copy-start | bytes 3076

commit v6 on v5

--- a/solution.py
+++ b/solution.py
@@ -57,21 +57,18 @@
     cut = units // TILE * TILE
     main, rest = slice(0, cut), slice(cut, units)
 
-    def project(lanes, *weights):
-        value = 0.0
-        for rank, columns in enumerate(slices):
-            rows = rows_ref[rank, :, :, lanes].reshape(total, width)
-            block = [ref[0, part, columns] for ref, part in weights]
-            block = block[0] if len(block) == 1 else jnp.concatenate(block, axis=0)
-            value = value + times_rows(rows, block)
-        return value
-
     first, second = slice(0, width), slice(width, 2 * width)
-    gate_main = project(first, (gate_ref, main))
-    up_main = project(first, (up_ref, main))
-    both_rest = project(first, (gate_ref, rest), (up_ref, rest))
-    back_main = project(second, (down_ref, main))
-    back_rest = project(second, (down_ref, rest))
+    gate_main = up_main = both_rest = turned = 0.0
+    for rank, columns in enumerate(slices):
+        rows_in = rows_ref[rank, :, :, first].reshape(total, width)
+        rows_back = rows_ref[rank, :, :, second].reshape(total, width)
+        both = jnp.concatenate([gate_ref[0, rest, columns], up_ref[0, rest, columns]], axis=0)
+        turned = turned + times_rows(down_ref[0, :, columns], rows_back)
+        gate_main = gate_main + times_rows(rows_in, gate_ref[0, main, columns])
+        up_main = up_main + times_rows(rows_in, up_ref[0, main, columns])
+        both_rest = both_rest + times_rows(rows_in, both)
+    back_proj = jnp.concatenate([turned, jnp.zeros((units, LANES - total), jnp.float32)], axis=1).T[:total]
+    back_main, back_rest = back_proj[:, main], back_proj[:, rest]
     product_main, by_gate_main, by_up_main = gradients(gate_main, up_main, back_main)
     product_rest, by_gate_rest, by_up_rest = gradients(
         both_rest[:, : units - cut], both_rest[:, units - cut :], back_rest
@@ -92,7 +89,6 @@
         for rank in range(rank_count):
             out_ref[rank, group, slots * (width // LANES) // 2] = tail.astype(jnp.bfloat16)
 
-    flat_ref = out_ref.reshape(rank_count, group_count, 2 * out_ref.shape[2], LANES)
     for rank, columns in enumerate(slices):
         weight_rest = jnp.concatenate([gate_ref[0, rest, columns], up_ref[0, rest, columns]], axis=0)
         partial = times_units(by_gate_main, gate_ref[0, main, columns])
@@ -103,12 +99,12 @@
             rows = slice(group * slots, (group + 1) * slots)
             for index in range(width // LANES):
                 lanes = slice(index * LANES, (index + 1) * LANES)
-                flat_ref[rank, group, index * slots : (index + 1) * slots, :] = partial[rows, lanes]
+                place = slice(index * slots // 2, (index + 1) * slots // 2)
+                out_ref[rank, group, place] = partial[rows, lanes].reshape(slots // 2, 2, LANES)
 
 
 def owner_kernel(parts_ref, routes_ref, weights_ref, grad_ref, gates_ref):
     rank_count, _, length, _, _ = parts_ref.shape
-    flat_ref = parts_ref.reshape(rank_count, parts_ref.shape[1], 2 * length, LANES)
     total, width = grad_ref.shape
     slots = total // rank_count
     body = slots * (width // LANES) // 2
@@ -121,12 +117,12 @@
     for rank in range(rank_count):
         rows = slice(rank * slots, (rank + 1) * slots)
         for index in range(width // LANES):
-            place = slice(index * slots, (index + 1) * slots)
+            place = slice(index * slots // 2, (index + 1) * slots // 2)
             value = 0.0
             for expert in range(TOP):
-                pair = flat_ref[rank, expert, place].astype(jnp.float32)
-                pair = pair + flat_ref[rank, expert + TOP, place].astype(jnp.float32)
-                value = value + scales[expert][rows] * pair
+                pair = parts_ref[rank, expert, place].astype(jnp.float32)
+                pair = pair + parts_ref[rank, expert + TOP, place].astype(jnp.float32)
+                value = value + scales[expert][rows] * pair.reshape(slots, LANES)
             grad_ref[rows, index * LANES : (index + 1) * LANES] = value.astype(jnp.bfloat16)
     owner = lax.broadcasted_iota(jnp.int32, (2, LANES), 1) // slots
     inner = []

time: 59.8 us -> 59.5 us (level)
  no operation moved by 1% of the time
where the time goes in v6:
time: 59.5 us; the launch traced here: 58.5 us
  blocking collectives  51.1 us (86%)
  Pallas kernels  4.9 us (8%)
  other arithmetic  1.14 us (2%)
  between operations  0.69 us (1%)
  starting transfers between devices  0.6 us (1%)
    all_to_all x1, blocking collectives, every_expert(): held = lax.all_to_all(send, both, split_axis=0, concat_axis=0, tiled=True)  32.1 us
    all_to_all x1, blocking collectives, every_expert(): lax.all_to_all(back, both, split_axis=0, concat_axis=0, tiled=True)  19 us
    pallas_call x1, Pallas kernels, every_expert(): pl.pallas_call(half_kernel, out_shape=jax.ShapeDtypeStruct((rank_count, g...  3.85 us
  transfers between devices with their start and end apart: 2, of which 0 were waited for; matrix products, arithmetic and copies ran while one was open for 0% of the time, Pallas kernels for 0%

profile of v6, /device:TPU:0, one launch (start us, length us, event | category | flops | bytes accessed | tf_op | source)
XLA Modules:
  0.0 58.5 jit_solution(3764333156030494690)
XLA Ops:
  0.6 0.0 copy-start
  0.6 1.1 %pad_maximum_fusion = bf16[128,1024]{1,0:T(8,128)(2,1)S(1)} fusion(bf16[128,512]{1,0:T(8,128)(2,1)} %param.8, bf16[128,512]{1,0:T(8,128)(2,1)} %param.7), kind=kLoop, calls=%fused_computation | loop fusion | flops 524288 | bytes 524288 | tf_op jit(solution)/shard_map/concatenate | solution.py:149
  1.8 0.1 broadcast_in_dim.8
  1.9 0.5 collective-permute-start
  2.4 0.1 collective-permute-start.1
  2.5 32.1 %all_to_all.10 = bf16[32,16,1024]{2,1,0:T(8,128)(2,1)S(1)} all-to-all(bf16[32,16,1024]{2,1,0:T(8,128)(2,1)S(1)} %bitcast.13), channel_id=1, replica_groups=mesh['grp'=4,'ep'=8] {'ep','grp'}, dimensions={0} | all-to-all | bytes 2097152 | tf_op jit(solution)/shard_map/all_to_all | solution.py:156
  34.6 0.0 collective-permute-done.up_ref
  34.6 0.0 collective-permute-done.1.down_ref
  34.6 0.0 copy-done
  34.7 0.0 copy-start.1
  34.7 0.0 copy-start.2
  34.7 3.9 %shard_map.86 = bf16[8,4,33,2,128]{4,3,2,1,0:T(2,128)(2,1)S(1)} custom-call(bf16[8,4,16,1024]{3,2,1,0:T(8,128)(2,1)S(1)} %bitcast.8, bf16[1,384,4096]{2,1,0:T(8,128)(2,1)S(1)} %copy-done, bf16[1,384,4096]{2,1,0:T(8,128)(2,1)S(1)} %collective-permute-done.up_ref, bf16[1,384,4096]{2,1,0:T(8,128)(2,1)S(1)} %collective-permute-done.1.down_ref), custom_call_target="tpu_custom_call" | custom-call | tf_op jit(solution)/shard_map/pallas_call | solution.py:157
  38.5 19.0 %all_to_all.11 = bf16[32,33,2,128]{3,2,1,0:T(2,128)(2,1)S(1)} all-to-all(bf16[32,33,2,128]{3,2,1,0:T(2,128)(2,1)S(1)} %bitcast.10), channel_id=1, replica_groups=mesh['grp'=4,'ep'=8] {'ep','grp'}, dimensions={0} | all-to-all | bytes 1081344 | tf_op jit(solution)/shard_map/all_to_all | solution.py:170
  57.5 0.0 copy-done.1
  57.5 0.0 copy-done.2
  57.5 1.1 %shard_map.87 = (bf16[128,512]{1,0:T(8,128)(2,1)}, f32[2,128]{1,0:T(2,128)}) custom-call(bf16[8,4,33,2,128]{4,3,2,1,0:T(2,128)(2,1)S(1)} %bitcast.9, s32[2,128]{1,0:T(2,128)S(1)} %bitcast.11, f32[2,128]{1,0:T(2,128)S(1)} %bitcast.12), custom_call_target="tpu_custom_call" | custom-call | tf_op jit(solution)/shard_map/pallas_call | solution.py:171
Async XLA Ops:
  0.6 34.0 %copy-start = (bf16[1,384,4096]{2,1,0:T(8,128)(2,1)S(1)}, bf16[1,384,4096]{2,1,0:T(8,128)(2,1)}, u32[]{:S(2)}) copy-start(bf16[1,384,4096]{2,1,0:T(8,128)(2,1)} %gate_ref.1) | copy-start | bytes 9437188
  1.9 32.7 %collective-permute-start = (bf16[1,384,4096]{2,1,0:T(8,128)(2,1)}, bf16[1,384,4096]{2,1,0:T(8,128)(2,1)S(1)}, u32[]{:S(2)}, u32[]{:S(2)}) collective-permute-start(bf16[1,384,4096]{2,1,0:T(8,128)(2,1)} %param.12), channel_id=1, source_target_pairs={{0,1},{1,0},{2,3},{3,2},{4,5},{5,4},{6,7},{7,6},{8,9},{9,8},{10,11... | collective-permute-start | bytes 9437192 | tf_op jit(solution)/shard_map/ppermute | solution.py:153
  2.4 32.2 %collective-permute-start.1 = (bf16[1,384,4096]{2,1,0:T(8,128)(2,1)}, bf16[1,384,4096]{2,1,0:T(8,128)(2,1)S(1)}, u32[]{:S(2)}, u32[]{:S(2)}) collective-permute-start(bf16[1,384,4096]{2,1,0:T(8,128)(2,1)} %param.13), channel_id=1, source_target_pairs={{0,1},{1,0},{2,3},{3,2},{4,5},{5,4},{6,7},{7,6},{8,9},{9,8},{10,11... | collective-permute-start | bytes 9437192 | tf_op jit(solution)/shard_map/ppermute | solution.py:154
  34.7 22.8 %copy-start.1 = (s32[128,2]{0,1:T(2,128)S(1)}, s32[128,2]{0,1:T(2,128)}, u32[]{:S(2)}) copy-start(s32[128,2]{0,1:T(2,128)} %param.9) | copy-start | bytes 3076
  34.7 22.8 %copy-start.2 = (f32[128,2]{0,1:T(2,128)S(1)}, f32[128,2]{0,1:T(2,128)}, u32[]{:S(2)}) copy-start(f32[128,2]{0,1:T(2,128)} %param.10) | copy-start | bytes 3076

commit v7 on v6

--- a/solution.py
+++ b/solution.py
@@ -1,14 +1,22 @@
+import functools
+import math
+
 import jax
 import jax.numpy as jnp
+import numpy as np
 from jax import lax
 from jax.experimental import pallas as pl
 from jax.experimental.pallas import tpu as pltpu
+from jax.sharding import Mesh
 from jax.sharding import PartitionSpec as P
 
 TOP = 2
 LANES = 128
 PARTS = 2
 TILE = 256
+RANK_AXES = ("ep_y", "ep_x", "ep_core")
+GROUP_AXES = ("grp_hi", "grp_lo")
+SEND_AXES = ("ep_x", "ep_y", "grp_hi", "ep_core", "grp_lo")
 VMEM_BYTES = 40 * 1024 * 1024
 
 
@@ -47,12 +55,28 @@
     return row
 
 
-def half_kernel(rows_ref, gate_ref, up_ref, down_ref, out_ref):
-    rank_count, group_count, slots, width = rows_ref.shape
+def pack_kernel(places, tokens_hbm, grad_hbm, out_ref, tokens_ref, grad_ref, arrived):
+    _, slots, width = out_ref.shape
+    lanes = (slice(0, width // 2), slice(width // 2, width))
+    copies = [
+        pltpu.make_async_copy(tokens_hbm, tokens_ref, arrived.at[0]),
+        pltpu.make_async_copy(grad_hbm, grad_ref, arrived.at[1]),
+    ]
+    for copy in copies:
+        copy.start()
+    for copy, source, half in zip(copies, (tokens_ref, grad_ref), lanes):
+        copy.wait()
+        for of_group in places:
+            for rank, place in enumerate(of_group):
+                out_ref[place, :, half] = source[rank * slots : (rank + 1) * slots, :]
+
+
+def half_kernel(places, rows_ref, gate_ref, up_ref, down_ref, out_ref):
+    group_count, rank_count = len(places), len(places[0])
+    _, slots, width = rows_ref.shape
     width = width // 2
     total = group_count * slots
     slices = [slice(rank * width, (rank + 1) * width) for rank in range(rank_count)]
-
     units = gate_ref.shape[1]
     cut = units // TILE * TILE
     main, rest = slice(0, cut), slice(cut, units)
@@ -60,8 +84,8 @@
     first, second = slice(0, width), slice(width, 2 * width)
     gate_main = up_main = both_rest = turned = 0.0
     for rank, columns in enumerate(slices):
-        rows_in = rows_ref[rank, :, :, first].reshape(total, width)
-        rows_back = rows_ref[rank, :, :, second].reshape(total, width)
+        rows_in = jnp.concatenate([rows_ref[of_group[rank], :, first] for of_group in places], axis=0)
+        rows_back = jnp.concatenate([rows_ref[of_group[rank], :, second] for of_group in places], axis=0)
         both = jnp.concatenate([gate_ref[0, rest, columns], up_ref[0, rest, columns]], axis=0)
         turned = turned + times_rows(down_ref[0, :, columns], rows_back)
         gate_main = gate_main + times_rows(rows_in, gate_ref[0, main, columns])
@@ -86,8 +110,8 @@
         tail = jnp.zeros((2, LANES), jnp.float32)
         for index, piece in enumerate(split_float(repeat_lanes(inner_sum, group * slots, slots))):
             tail = jnp.where(line == index, piece, tail)
-        for rank in range(rank_count):
-            out_ref[rank, group, slots * (width // LANES) // 2] = tail.astype(jnp.bfloat16)
+        for place in places[group]:
+            out_ref[place, slots * (width // LANES) // 2] = tail.astype(jnp.bfloat16)
 
     for rank, columns in enumerate(slices):
         weight_rest = jnp.concatenate([gate_ref[0, rest, columns], up_ref[0, rest, columns]], axis=0)
@@ -99,14 +123,14 @@
             rows = slice(group * slots, (group + 1) * slots)
             for index in range(width // LANES):
                 lanes = slice(index * LANES, (index + 1) * LANES)
-                place = slice(index * slots // 2, (index + 1) * slots // 2)
-                out_ref[rank, group, place] = partial[rows, lanes].reshape(slots // 2, 2, LANES)
-
-
-def owner_kernel(parts_ref, routes_ref, weights_ref, grad_ref, gates_ref):
-    rank_count, _, length, _, _ = parts_ref.shape
+                pairs = slice(index * slots // 2, (index + 1) * slots // 2)
+                out_ref[places[group][rank], pairs] = partial[rows, lanes].reshape(slots // 2, 2, LANES)
+
+
+def owner_kernel(places, parts_ref, routes_ref, weights_ref, grad_ref, gates_ref):
+    count, length, _, _ = parts_ref.shape
     total, width = grad_ref.shape
-    slots = total // rank_count
+    slots = total // len(places[0])
     body = slots * (width // LANES) // 2
     first = routes_ref[:1, :] == 0
     scale_first = jnp.where(first, weights_ref[:1, :], weights_ref[1:, :])
@@ -114,62 +138,78 @@
     line = lax.broadcasted_iota(jnp.int32, (LANES, total), 0)
     turned = jnp.where(line == 0, scale_first, scale_second).T
     scales = (turned[:, :1], turned[:, 1:2])
-    for rank in range(rank_count):
+    for rank in range(len(places[0])):
         rows = slice(rank * slots, (rank + 1) * slots)
         for index in range(width // LANES):
-            place = slice(index * slots // 2, (index + 1) * slots // 2)
+            pairs = slice(index * slots // 2, (index + 1) * slots // 2)
             value = 0.0
             for expert in range(TOP):
-                pair = parts_ref[rank, expert, place].astype(jnp.float32)
-                pair = pair + parts_ref[rank, expert + TOP, place].astype(jnp.float32)
+                pair = parts_ref[places[expert][rank], pairs].astype(jnp.float32)
+                pair = pair + parts_ref[places[expert + TOP][rank], pairs].astype(jnp.float32)
                 value = value + scales[expert][rows] * pair.reshape(slots, LANES)
             grad_ref[rows, index * LANES : (index + 1) * LANES] = value.astype(jnp.bfloat16)
     owner = lax.broadcasted_iota(jnp.int32, (2, LANES), 1) // slots
     inner = []
     for expert in range(TOP):
         value = jnp.zeros((2, LANES), jnp.float32)
-        for rank in range(rank_count):
-            pair = parts_ref[rank, expert, body].astype(jnp.float32)
-            pair = pair + parts_ref[rank, expert + TOP, body].astype(jnp.float32)
+        for rank in range(len(places[0])):
+            pair = parts_ref[places[expert][rank], body].astype(jnp.float32)
+            pair = pair + parts_ref[places[expert + TOP][rank], body].astype(jnp.float32)
             value = value + jnp.where(owner == rank, pair, 0.0)
         inner.append(jnp.sum(value, axis=0, keepdims=True))
     gates_ref[...] = jnp.where(routes_ref[...] == 0, inner[0], inner[1])
 
 
+def message_places(order):
+    axes = GROUP_AXES + RANK_AXES
+    sizes = [lax.axis_size(axis) for axis in axes]
+    linear = np.arange(math.prod(sizes)).reshape([lax.axis_size(axis) for axis in order])
+    linear = linear.transpose([order.index(axis) for axis in axes])
+    return linear.reshape(sizes[0] * sizes[1], -1).tolist()
+
+
 def every_expert(tokens, grad_out, routes, route_weights, gate_weight, up_weight, down_weight):
-    group_count = lax.axis_size("grp")
-    rank_count = lax.axis_size("ep")
-    both = ("ep", "grp")
+    rank_count = lax.axis_size(RANK_AXES)
+    count = lax.axis_size(SEND_AXES)
     group_tokens, width = tokens.shape
     slots = group_tokens // rank_count
     length = slots * (width // LANES) // 2 + 1
     whole = pl.BlockSpec(memory_space=pltpu.VMEM)
+    there = pl.BlockSpec(memory_space=pltpu.HBM)
     params = pltpu.CompilerParams(vmem_limit_bytes=VMEM_BYTES)
-
-    paired = jnp.concatenate([tokens, grad_out], axis=1).reshape(rank_count, 1, slots, 2 * width)
-    send = jnp.broadcast_to(paired, (rank_count, group_count, slots, 2 * width))
-    swap = [(source, source ^ 1) for source in range(rank_count)]
+    places = message_places(SEND_AXES)
+
+    send = pl.pallas_call(
+        functools.partial(pack_kernel, places),
+        out_shape=jax.ShapeDtypeStruct((count, slots, 2 * width), tokens.dtype),
+        in_specs=[there] * 2,
+        out_specs=whole,
+        scratch_shapes=[
+            pltpu.VMEM(tokens.shape, tokens.dtype),
+            pltpu.VMEM(tokens.shape, tokens.dtype),
+            pltpu.SemaphoreType.DMA((2,)),
+        ],
+        compiler_params=params,
+    )(*[pltpu.with_memory_space_constraint(value, pltpu.HBM) for value in (tokens, grad_out)])
     send, up_weight, down_weight = lax.optimization_barrier((send, up_weight, down_weight))
-    up_weight = lax.ppermute(up_weight, "ep", swap)
-    down_weight = lax.ppermute(down_weight, "ep", swap)
-    send = send.reshape(group_count * rank_count, slots, 2 * width)
-    held = lax.all_to_all(send, both, split_axis=0, concat_axis=0, tiled=True)
+    up_weight = lax.ppermute(up_weight, RANK_AXES[-1], [(0, 1), (1, 0)])
+    down_weight = lax.ppermute(down_weight, RANK_AXES[-1], [(0, 1), (1, 0)])
+    held = lax.all_to_all(send, SEND_AXES, split_axis=0, concat_axis=0, tiled=True)
     back = pl.pallas_call(
-        half_kernel,
-        out_shape=jax.ShapeDtypeStruct((rank_count, group_count, length, 2, LANES), jnp.bfloat16),
+        functools.partial(half_kernel, places),
+        out_shape=jax.ShapeDtypeStruct((count, length, 2, LANES), jnp.bfloat16),
         in_specs=[whole] * 4,
         out_specs=whole,
         compiler_params=params,
     )(
-        held.reshape(rank_count, group_count, slots, 2 * width),
+        held,
         gate_weight,
         up_weight,
         down_weight,
     )
-    back = back.reshape(group_count * rank_count, length, 2, LANES)
-    arrived = lax.all_to_all(back, both, split_axis=0, concat_axis=0, tiled=True)
+    arrived = lax.all_to_all(back, SEND_AXES, split_axis=0, concat_axis=0, tiled=True)
     grad_tokens, grad_gates = pl.pallas_call(
-        owner_kernel,
+        functools.partial(owner_kernel, places),
         out_shape=(
             jax.ShapeDtypeStruct(tokens.shape, jnp.bfloat16),
             jax.ShapeDtypeStruct((TOP, group_tokens), jnp.float32),
@@ -177,7 +217,7 @@
         in_specs=[whole] * 3,
         out_specs=(whole, whole),
         compiler_params=params,
-    )(arrived.reshape(rank_count, group_count, length, 2, LANES), routes.T, route_weights.T)
+    )(arrived, routes.T, route_weights.T)
     return grad_tokens, grad_gates.T
 
 
@@ -240,26 +280,23 @@
     return (grad_tokens.astype(jnp.bfloat16), grad_gates)
 
 
-def on_device(*args):
-    everywhere = lax.axis_size("grp") // 2 == TOP and args[0].shape[0] == LANES
-    everywhere = everywhere and lax.axis_size("ep") % 2 == 0
-    return every_expert(*args) if everywhere else by_slots(*args)
-
-
 def solution(mesh):
-    placed = (
-        P("grp", "ep"),
-        P("grp", "ep"),
-        P("grp", None),
-        P("grp", None),
-        P("grp", None, None),
-        P("grp", None, None),
-        P("grp", None, None),
-    )
-    return jax.shard_map(
-        on_device,
-        mesh=mesh,
-        in_specs=placed,
-        out_specs=(P("grp", "ep"), P("grp", None)),
-        check_vma=False,
-    )
+    groups, ranks = mesh.shape["grp"], mesh.shape["ep"]
+
+    def run(tokens, *others):
+        everywhere = groups == 2 * TOP and tokens.shape[0] == groups * LANES and ranks == 8
+        if everywhere:
+            fine = Mesh(mesh.devices.reshape([2] * 5), GROUP_AXES + RANK_AXES)
+            placed, body, axes, grp = fine, every_expert, RANK_AXES, GROUP_AXES
+        else:
+            placed, body, axes, grp = mesh, by_slots, "ep", "grp"
+        weights = [P(grp, None, None)] * 3
+        return jax.shard_map(
+            body,
+            mesh=placed,
+            in_specs=(P(grp, axes), P(grp, axes), P(grp, None), P(grp, None), *weights),
+            out_specs=(P(grp, axes), P(grp, None)),
+            check_vma=False,
+        )(tokens, *others)
+
+    return run

time: 59.5 us -> 58.9 us (0.990); the launches traced: 58.5 us -> 58.7 us
  Pallas kernels: 4.9 us -> 6.08 us
  other arithmetic: 1.14 us -> 0 us
    pallas_call x2 -> x3, Pallas kernels: 4.9 us -> 6.08 us  [the longest x1 3.86 us: every_expert(): pl.pallas_call(functools.partial(half_kernel, places), out_shape=jax.Shap...]
    concatenate x1 -> x0, other arithmetic: 1.14 us -> none  [every_expert(): jnp.concatenate([tokens, grad_out], axis=1)]
where the time goes in v7:
time: 58.9 us; the launch traced here: 58.7 us
  blocking collectives  51.3 us (87%)
  Pallas kernels  6.08 us (10%)
  between operations  0.67 us (1%)
  starting transfers between devices  0.6 us (1%)
    all_to_all x1, blocking collectives, every_expert(): lax.all_to_all(send, SEND_AXES, split_axis=0, concat_axis=0, tiled=True)  31.4 us
    all_to_all x1, blocking collectives, every_expert(): lax.all_to_all(back, SEND_AXES, split_axis=0, concat_axis=0, tiled=True)  19.9 us
    pallas_call x1, Pallas kernels, every_expert(): pl.pallas_call(functools.partial(half_kernel, places), out_shape=jax.Shap...  3.86 us
  transfers between devices with their start and end apart: 2, of which 0 were waited for; matrix products, arithmetic and copies ran while one was open for 0% of the time, Pallas kernels for 0%

profile of v7, /device:TPU:0, one launch (start us, length us, event | category | flops | bytes accessed | tf_op | source)
XLA Modules:
  0.0 58.7 jit_solution(16511843367216219842)
XLA Ops:
  0.6 0.0 copy-start
  0.6 1.2 %shard_map.86 = bf16[32,16,1024]{2,1,0:T(8,128)(2,1)S(1)} custom-call(bf16[128,512]{1,0:T(8,128)(2,1)} %tokens_hbm.1, bf16[128,512]{1,0:T(8,128)(2,1)} %grad_hbm.1), custom_call_target="tpu_custom_call" | custom-call | tf_op jit(solution)/shard_map/pallas_call | solution.py:182
  1.8 0.5 collective-permute-start
  2.3 0.1 collective-permute-start.1
  2.4 31.4 %all_to_all.10.rows_ref = bf16[32,16,1024]{2,1,0:T(8,128)(2,1)S(1)} all-to-all(bf16[32,16,1024]{2,1,0:T(8,128)(2,1)S(1)} %shard_map.86), channel_id=1, replica_groups=mesh['grp_hi'=2,'grp_lo'=2,'ep_y'=2,'ep_x'=2,'ep_core'=2] {'ep_x','ep_y'..., dimensions={0} | all-to-all | bytes 2097152 | tf_op jit(solution)/shard_map/all_to_all | solution.py:197
  33.8 0.0 copy-start.1
  33.9 0.0 copy-start.2
  33.9 0.0 collective-permute-done.up_ref
  33.9 0.0 collective-permute-done.1.down_ref
  33.9 0.0 copy-done
  33.9 3.9 %shard_map.87 = bf16[32,33,2,128]{3,2,1,0:T(2,128)(2,1)S(1)} custom-call(bf16[32,16,1024]{2,1,0:T(8,128)(2,1)S(1)} %all_to_all.10.rows_ref, bf16[1,384,4096]{2,1,0:T(8,128)(2,1)S(1)} %copy-done, bf16[1,384,4096]{2,1,0:T(8,128)(2,1)S(1)} %collective-permute-done.up_ref, bf16[1,384,4096]{2,1,0:T(8,128)(2,1)S(1)} %collective-permute-done.1.down_ref), custom_call_target="tpu_custom_call" | custom-call | tf_op jit(solution)/shard_map/pallas_call | solution.py:198
  37.7 19.9 %all_to_all.11.parts_ref = bf16[32,33,2,128]{3,2,1,0:T(2,128)(2,1)S(1)} all-to-all(bf16[32,33,2,128]{3,2,1,0:T(2,128)(2,1)S(1)} %shard_map.87), channel_id=1, replica_groups=mesh['grp_hi'=2,'grp_lo'=2,'ep_y'=2,'ep_x'=2,'ep_core'=2] {'ep_x','ep_y'..., dimensions={0} | all-to-all | bytes 1081344 | tf_op jit(solution)/shard_map/all_to_all | solution.py:210
  57.6 0.0 copy-done.1
  57.6 0.0 copy-done.2
  57.6 1.1 %shard_map.88 = (bf16[128,512]{1,0:T(8,128)(2,1)}, f32[2,128]{1,0:T(2,128)}) custom-call(bf16[32,33,2,128]{3,2,1,0:T(2,128)(2,1)S(1)} %all_to_all.11.parts_ref, s32[2,128]{1,0:T(2,128)S(1)} %bitcast.3, f32[2,128]{1,0:T(2,128)S(1)} %bitcast.4), custom_call_target="tpu_custom_call" | custom-call | tf_op jit(solution)/shard_map/pallas_call | solution.py:211
Async XLA Ops:
  0.6 33.2 %copy-start = (bf16[1,384,4096]{2,1,0:T(8,128)(2,1)S(1)}, bf16[1,384,4096]{2,1,0:T(8,128)(2,1)}, u32[]{:S(2)}) copy-start(bf16[1,384,4096]{2,1,0:T(8,128)(2,1)} %gate_ref.1) | copy-start | bytes 9437188
  1.8 32.0 %collective-permute-start = (bf16[1,384,4096]{2,1,0:T(8,128)(2,1)}, bf16[1,384,4096]{2,1,0:T(8,128)(2,1)S(1)}, u32[]{:S(2)}, u32[]{:S(2)}) collective-permute-start(bf16[1,384,4096]{2,1,0:T(8,128)(2,1)} %param.12), channel_id=1, source_target_pairs={{0,1},{1,0},{2,3},{3,2},{4,5},{5,4},{6,7},{7,6},{8,9},{9,8},{10,11... | collective-permute-start | bytes 9437192 | tf_op jit(solution)/shard_map/ppermute | solution.py:195
  2.3 31.5 %collective-permute-start.1 = (bf16[1,384,4096]{2,1,0:T(8,128)(2,1)}, bf16[1,384,4096]{2,1,0:T(8,128)(2,1)S(1)}, u32[]{:S(2)}, u32[]{:S(2)}) collective-permute-start(bf16[1,384,4096]{2,1,0:T(8,128)(2,1)} %param.13), channel_id=1, source_target_pairs={{0,1},{1,0},{2,3},{3,2},{4,5},{5,4},{6,7},{7,6},{8,9},{9,8},{10,11... | collective-permute-start | bytes 9437192 | tf_op jit(solution)/shard_map/ppermute | solution.py:196
  33.8 23.8 %copy-start.1 = (s32[128,2]{0,1:T(2,128)S(1)}, s32[128,2]{0,1:T(2,128)}, u32[]{:S(2)}) copy-start(s32[128,2]{0,1:T(2,128)} %param.9) | copy-start | bytes 3076
  33.9 23.8 %copy-start.2 = (f32[128,2]{0,1:T(2,128)S(1)}, f32[128,2]{0,1:T(2,128)}, u32[]{:S(2)}) copy-start(f32[128,2]{0,1:T(2,128)} %param.10) | copy-start | bytes 3076

commit v8 on v7

--- a/solution.py
+++ b/solution.py
@@ -81,14 +81,16 @@
     cut = units // TILE * TILE
     main, rest = slice(0, cut), slice(cut, units)
 
-    first, second = slice(0, width), slice(width, 2 * width)
     gate_main = up_main = both_rest = turned = 0.0
-    for rank, columns in enumerate(slices):
+    for at in range(0, rank_count * width, TILE):
+        rank, start = divmod(at, width)
+        columns = slice(at, at + TILE)
+        first, second = slice(start, start + TILE), slice(width + start, width + start + TILE)
         rows_in = jnp.concatenate([rows_ref[of_group[rank], :, first] for of_group in places], axis=0)
         rows_back = jnp.concatenate([rows_ref[of_group[rank], :, second] for of_group in places], axis=0)
         both = jnp.concatenate([gate_ref[0, rest, columns], up_ref[0, rest, columns]], axis=0)
+        gate_main = gate_main + times_rows(rows_in, gate_ref[0, main, columns])
         turned = turned + times_rows(down_ref[0, :, columns], rows_back)
-        gate_main = gate_main + times_rows(rows_in, gate_ref[0, main, columns])
         up_main = up_main + times_rows(rows_in, up_ref[0, main, columns])
         both_rest = both_rest + times_rows(rows_in, both)
     back_proj = jnp.concatenate([turned, jnp.zeros((units, LANES - total), jnp.float32)], axis=1).T[:total]

time: 58.9 us -> 58.6 us (level)
  no operation moved by 1% of the time
where the time goes in v8:
time: 58.6 us; the launch traced here: 58.5 us
  blocking collectives  51.3 us (88%)
  Pallas kernels  5.85 us (10%)
  between operations  0.67 us (1%)
  starting transfers between devices  0.6 us (1%)
    all_to_all x1, blocking collectives, every_expert(): lax.all_to_all(send, SEND_AXES, split_axis=0, concat_axis=0, tiled=True)  31.4 us
    all_to_all x1, blocking collectives, every_expert(): lax.all_to_all(back, SEND_AXES, split_axis=0, concat_axis=0, tiled=True)  19.9 us
    pallas_call x1, Pallas kernels, every_expert(): pl.pallas_call(functools.partial(half_kernel, places), out_shape=jax.Shap...  3.63 us
    pallas_call x1, Pallas kernels, every_expert(): pl.pallas_call(functools.partial(pack_kernel, places), out_shape=jax.Shap...  1.18 us
  transfers between devices with their start and end apart: 2, of which 0 were waited for; matrix products, arithmetic and copies ran while one was open for 0% of the time, Pallas kernels for 0%

profile of v8, /device:TPU:0, one launch (start us, length us, event | category | flops | bytes accessed | tf_op | source)
XLA Modules:
  0.0 58.5 jit_solution(9043726241079510751)
XLA Ops:
  0.6 0.0 copy-start
  0.6 1.2 %shard_map.86 = bf16[32,16,1024]{2,1,0:T(8,128)(2,1)S(1)} custom-call(bf16[128,512]{1,0:T(8,128)(2,1)} %tokens_hbm.1, bf16[128,512]{1,0:T(8,128)(2,1)} %grad_hbm.1), custom_call_target="tpu_custom_call" | custom-call | tf_op jit(solution)/shard_map/pallas_call | solution.py:184
  1.8 0.5 collective-permute-start
  2.3 0.1 collective-permute-start.1
  2.4 31.4 %all_to_all.10.rows_ref = bf16[32,16,1024]{2,1,0:T(8,128)(2,1)S(1)} all-to-all(bf16[32,16,1024]{2,1,0:T(8,128)(2,1)S(1)} %shard_map.86), channel_id=1, replica_groups=mesh['grp_hi'=2,'grp_lo'=2,'ep_y'=2,'ep_x'=2,'ep_core'=2] {'ep_x','ep_y'..., dimensions={0} | all-to-all | bytes 2097152 | tf_op jit(solution)/shard_map/all_to_all | solution.py:199
  33.8 0.0 copy-start.1
  33.9 0.0 copy-start.2
  33.9 0.0 collective-permute-done.up_ref
  33.9 0.0 collective-permute-done.1.down_ref
  33.9 0.0 copy-done
  33.9 3.6 %shard_map.87 = bf16[32,33,2,128]{3,2,1,0:T(2,128)(2,1)S(1)} custom-call(bf16[32,16,1024]{2,1,0:T(8,128)(2,1)S(1)} %all_to_all.10.rows_ref, bf16[1,384,4096]{2,1,0:T(8,128)(2,1)S(1)} %copy-done, bf16[1,384,4096]{2,1,0:T(8,128)(2,1)S(1)} %collective-permute-done.up_ref, bf16[1,384,4096]{2,1,0:T(8,128)(2,1)S(1)} %collective-permute-done.1.down_ref), custom_call_target="tpu_custom_call" | custom-call | tf_op jit(solution)/shard_map/pallas_call | solution.py:200
  37.5 19.9 %all_to_all.11.parts_ref = bf16[32,33,2,128]{3,2,1,0:T(2,128)(2,1)S(1)} all-to-all(bf16[32,33,2,128]{3,2,1,0:T(2,128)(2,1)S(1)} %shard_map.87), channel_id=1, replica_groups=mesh['grp_hi'=2,'grp_lo'=2,'ep_y'=2,'ep_x'=2,'ep_core'=2] {'ep_x','ep_y'..., dimensions={0} | all-to-all | bytes 1081344 | tf_op jit(solution)/shard_map/all_to_all | solution.py:212
  57.4 0.0 copy-done.1
  57.4 0.0 copy-done.2
  57.4 1.1 %shard_map.88 = (bf16[128,512]{1,0:T(8,128)(2,1)}, f32[2,128]{1,0:T(2,128)}) custom-call(bf16[32,33,2,128]{3,2,1,0:T(2,128)(2,1)S(1)} %all_to_all.11.parts_ref, s32[2,128]{1,0:T(2,128)S(1)} %bitcast.3, f32[2,128]{1,0:T(2,128)S(1)} %bitcast.4), custom_call_target="tpu_custom_call" | custom-call | tf_op jit(solution)/shard_map/pallas_call | solution.py:213
Async XLA Ops:
  0.6 33.2 %copy-start = (bf16[1,384,4096]{2,1,0:T(8,128)(2,1)S(1)}, bf16[1,384,4096]{2,1,0:T(8,128)(2,1)}, u32[]{:S(2)}) copy-start(bf16[1,384,4096]{2,1,0:T(8,128)(2,1)} %gate_ref.1) | copy-start | bytes 9437188
  1.8 32.0 %collective-permute-start = (bf16[1,384,4096]{2,1,0:T(8,128)(2,1)}, bf16[1,384,4096]{2,1,0:T(8,128)(2,1)S(1)}, u32[]{:S(2)}, u32[]{:S(2)}) collective-permute-start(bf16[1,384,4096]{2,1,0:T(8,128)(2,1)} %param.12), channel_id=1, source_target_pairs={{0,1},{1,0},{2,3},{3,2},{4,5},{5,4},{6,7},{7,6},{8,9},{9,8},{10,11... | collective-permute-start | bytes 9437192 | tf_op jit(solution)/shard_map/ppermute | solution.py:197
  2.3 31.5 %collective-permute-start.1 = (bf16[1,384,4096]{2,1,0:T(8,128)(2,1)}, bf16[1,384,4096]{2,1,0:T(8,128)(2,1)S(1)}, u32[]{:S(2)}, u32[]{:S(2)}) collective-permute-start(bf16[1,384,4096]{2,1,0:T(8,128)(2,1)} %param.13), channel_id=1, source_target_pairs={{0,1},{1,0},{2,3},{3,2},{4,5},{5,4},{6,7},{7,6},{8,9},{9,8},{10,11... | collective-permute-start | bytes 9437192 | tf_op jit(solution)/shard_map/ppermute | solution.py:198
  33.8 23.6 %copy-start.1 = (s32[128,2]{0,1:T(2,128)S(1)}, s32[128,2]{0,1:T(2,128)}, u32[]{:S(2)}) copy-start(s32[128,2]{0,1:T(2,128)} %param.9) | copy-start | bytes 3076
  33.9 23.6 %copy-start.2 = (f32[128,2]{0,1:T(2,128)S(1)}, f32[128,2]{0,1:T(2,128)}, u32[]{:S(2)}) copy-start(f32[128,2]{0,1:T(2,128)} %param.10) | copy-start | bytes 3076

commit v9 on v8

--- a/solution.py
+++ b/solution.py
@@ -71,7 +71,7 @@
                 out_ref[place, :, half] = source[rank * slots : (rank + 1) * slots, :]
 
 
-def half_kernel(places, rows_ref, gate_ref, up_ref, down_ref, out_ref):
+def half_kernel(places, rows_ref, gate_ref, up_ref, down_ref, routes_ref, weights_ref, out_ref, scales_ref):
     group_count, rank_count = len(places), len(places[0])
     _, slots, width = rows_ref.shape
     width = width // 2
@@ -102,6 +102,11 @@
     product = jnp.concatenate([product_main, product_rest], axis=1)
     by_rest = jnp.concatenate([by_gate_rest, by_up_rest], axis=1)
 
+    taken = routes_ref[:1, :] == 0
+    for expert, (one, other) in enumerate(((0, 1), (1, 0))):
+        factor = jnp.where(taken, weights_ref[one : one + 1, :], weights_ref[other : other + 1, :])
+        scales_ref[expert] = jnp.broadcast_to(factor, (LANES, LANES)).T
+
     folded = product[:, :LANES]
     for start in range(LANES, product.shape[1], LANES):
         folded = folded + product[:, start : start + LANES]
@@ -129,17 +134,11 @@
                 out_ref[places[group][rank], pairs] = partial[rows, lanes].reshape(slots // 2, 2, LANES)
 
 
-def owner_kernel(places, parts_ref, routes_ref, weights_ref, grad_ref, gates_ref):
+def owner_kernel(places, parts_ref, routes_ref, scales_ref, grad_ref, gates_ref):
     count, length, _, _ = parts_ref.shape
     total, width = grad_ref.shape
     slots = total // len(places[0])
     body = slots * (width // LANES) // 2
-    first = routes_ref[:1, :] == 0
-    scale_first = jnp.where(first, weights_ref[:1, :], weights_ref[1:, :])
-    scale_second = jnp.where(first, weights_ref[1:, :], weights_ref[:1, :])
-    line = lax.broadcasted_iota(jnp.int32, (LANES, total), 0)
-    turned = jnp.where(line == 0, scale_first, scale_second).T
-    scales = (turned[:, :1], turned[:, 1:2])
     for rank in range(len(places[0])):
         rows = slice(rank * slots, (rank + 1) * slots)
         for index in range(width // LANES):
@@ -148,7 +147,7 @@
             for expert in range(TOP):
                 pair = parts_ref[places[expert][rank], pairs].astype(jnp.float32)
                 pair = pair + parts_ref[places[expert + TOP][rank], pairs].astype(jnp.float32)
-                value = value + scales[expert][rows] * pair.reshape(slots, LANES)
+                value = value + scales_ref[expert, rows, :] * pair.reshape(slots, LANES)
             grad_ref[rows, index * LANES : (index + 1) * LANES] = value.astype(jnp.bfloat16)
     owner = lax.broadcasted_iota(jnp.int32, (2, LANES), 1) // slots
     inner = []
@@ -197,17 +196,22 @@
     up_weight = lax.ppermute(up_weight, RANK_AXES[-1], [(0, 1), (1, 0)])
     down_weight = lax.ppermute(down_weight, RANK_AXES[-1], [(0, 1), (1, 0)])
     held = lax.all_to_all(send, SEND_AXES, split_axis=0, concat_axis=0, tiled=True)
-    back = pl.pallas_call(
+    back, scales = pl.pallas_call(
         functools.partial(half_kernel, places),
-        out_shape=jax.ShapeDtypeStruct((count, length, 2, LANES), jnp.bfloat16),
-        in_specs=[whole] * 4,
-        out_specs=whole,
+        out_shape=(
+            jax.ShapeDtypeStruct((count, length, 2, LANES), jnp.bfloat16),
+            jax.ShapeDtypeStruct((TOP, group_tokens, LANES), jnp.float32),
+        ),
+        in_specs=[whole] * 6,
+        out_specs=(whole, whole),
         compiler_params=params,
     )(
         held,
         gate_weight,
         up_weight,
         down_weight,
+        routes.T,
+        route_weights.T,
     )
     arrived = lax.all_to_all(back, SEND_AXES, split_axis=0, concat_axis=0, tiled=True)
     grad_tokens, grad_gates = pl.pallas_call(
@@ -219,7 +223,7 @@
         in_specs=[whole] * 3,
         out_specs=(whole, whole),
         compiler_params=params,
-    )(arrived, routes.T, route_weights.T)
+    )(arrived, routes.T, scales)
     return grad_tokens, grad_gates.T
 
 

time: 58.6 us -> 58.6 us (level)
  no operation moved by 1% of the time
where the time goes in v9:
time: 58.6 us; the launch traced here: 58.4 us
  blocking collectives  51.3 us (88%)
  Pallas kernels  5.8 us (10%)
  between operations  0.69 us (1%)
  starting transfers between devices  0.6 us (1%)
    all_to_all x1, blocking collectives, every_expert(): lax.all_to_all(send, SEND_AXES, split_axis=0, concat_axis=0, tiled=True)  31.4 us
    all_to_all x1, blocking collectives, every_expert(): lax.all_to_all(back, SEND_AXES, split_axis=0, concat_axis=0, tiled=True)  19.9 us
    pallas_call x1, Pallas kernels, every_expert(): pl.pallas_call(functools.partial(half_kernel, places), out_shape=(jax.Sha...  3.64 us
    pallas_call x1, Pallas kernels, every_expert(): pl.pallas_call(functools.partial(pack_kernel, places), out_shape=jax.Shap...  1.18 us
  transfers between devices with their start and end apart: 2, of which 0 were waited for; matrix products, arithmetic and copies ran while one was open for 0% of the time, Pallas kernels for 0%

profile of v9, /device:TPU:0, one launch (start us, length us, event | category | flops | bytes accessed | tf_op | source)
XLA Modules:
  0.0 58.4 jit_solution(3913248641959386294)
XLA Ops:
  0.6 0.0 copy-start
  0.6 0.0 copy-start.2
  0.7 0.0 copy-start.1
  0.7 1.2 %shard_map.86 = bf16[32,16,1024]{2,1,0:T(8,128)(2,1)S(1)} custom-call(bf16[128,512]{1,0:T(8,128)(2,1)} %tokens_hbm.1, bf16[128,512]{1,0:T(8,128)(2,1)} %grad_hbm.1), custom_call_target="tpu_custom_call" | custom-call | tf_op jit(solution)/shard_map/pallas_call | solution.py:183
  1.8 0.5 collective-permute-start
  2.4 0.1 collective-permute-start.1
  2.4 31.4 %all_to_all.10.rows_ref = bf16[32,16,1024]{2,1,0:T(8,128)(2,1)S(1)} all-to-all(bf16[32,16,1024]{2,1,0:T(8,128)(2,1)S(1)} %shard_map.86), channel_id=1, replica_groups=mesh['grp_hi'=2,'grp_lo'=2,'ep_y'=2,'ep_x'=2,'ep_core'=2] {'ep_x','ep_y'..., dimensions={0} | all-to-all | bytes 2097152 | tf_op jit(solution)/shard_map/all_to_all | solution.py:198
  33.9 0.0 collective-permute-done.up_ref
  33.9 0.0 collective-permute-done.1.down_ref
  33.9 0.0 copy-done
  33.9 0.0 copy-done.2
  33.9 0.0 copy-done.1
  33.9 3.6 %shard_map.87 = (bf16[32,33,2,128]{3,2,1,0:T(2,128)(2,1)S(1)}, f32[2,128,128]{2,1,0:T(8,128)S(1)}) custom-call(bf16[32,16,1024]{2,1,0:T(8,128)(2,1)S(1)} %all_to_all.10.rows_ref, bf16[1,384,4096]{2,1,0:T(8,128)(2,1)S(1)} %copy-done, bf16[1,384,4096]{2,1,0:T(8,128)(2,1)S(1)} %collective-permute-done.up_ref, ...), custom_call_target="tpu_custom_call" | custom-call | tf_op jit(solution)/shard_map/pallas_call | solution.py:199
  37.6 19.9 %all_to_all.11.parts_ref = bf16[32,33,2,128]{3,2,1,0:T(2,128)(2,1)S(1)} all-to-all(bf16[32,33,2,128]{3,2,1,0:T(2,128)(2,1)S(1)} %get-tuple-element.12), channel_id=1, replica_groups=mesh['grp_hi'=2,'grp_lo'=2,'ep_y'=2,'ep_x'=2,'ep_core'=2] {'ep_x','ep_y'..., dimensions={0} | all-to-all | bytes 1081344 | tf_op jit(solution)/shard_map/all_to_all | solution.py:216
  57.5 1.0 %shard_map.88 = (bf16[128,512]{1,0:T(8,128)(2,1)}, f32[2,128]{1,0:T(2,128)}) custom-call(bf16[32,33,2,128]{3,2,1,0:T(2,128)(2,1)S(1)} %all_to_all.11.parts_ref, s32[2,128]{1,0:T(2,128)S(1)} %bitcast.4, f32[2,128,128]{2,1,0:T(8,128)S(1)} %get-tuple-element.13.scales_ref), custom_call_target="tpu_custom_call" | custom-call | tf_op jit(solution)/shard_map/pallas_call | solution.py:217
Async XLA Ops:
  0.6 33.2 %copy-start = (bf16[1,384,4096]{2,1,0:T(8,128)(2,1)S(1)}, bf16[1,384,4096]{2,1,0:T(8,128)(2,1)}, u32[]{:S(2)}) copy-start(bf16[1,384,4096]{2,1,0:T(8,128)(2,1)} %gate_ref.1) | copy-start | bytes 9437188
  0.6 33.2 %copy-start.2 = (f32[128,2]{0,1:T(2,128)S(1)}, f32[128,2]{0,1:T(2,128)}, u32[]{:S(2)}) copy-start(f32[128,2]{0,1:T(2,128)} %param.10) | copy-start | bytes 3076
  0.7 33.2 %copy-start.1 = (s32[128,2]{0,1:T(2,128)S(1)}, s32[128,2]{0,1:T(2,128)}, u32[]{:S(2)}) copy-start(s32[128,2]{0,1:T(2,128)} %param.9) | copy-start | bytes 3076
  1.8 32.0 %collective-permute-start = (bf16[1,384,4096]{2,1,0:T(8,128)(2,1)}, bf16[1,384,4096]{2,1,0:T(8,128)(2,1)S(1)}, u32[]{:S(2)}, u32[]{:S(2)}) collective-permute-start(bf16[1,384,4096]{2,1,0:T(8,128)(2,1)} %param.12), channel_id=1, source_target_pairs={{0,1},{1,0},{2,3},{3,2},{4,5},{5,4},{6,7},{7,6},{8,9},{9,8},{10,11... | collective-permute-start | bytes 9437192 | tf_op jit(solution)/shard_map/ppermute | solution.py:196
  2.4 31.5 %collective-permute-start.1 = (bf16[1,384,4096]{2,1,0:T(8,128)(2,1)}, bf16[1,384,4096]{2,1,0:T(8,128)(2,1)S(1)}, u32[]{:S(2)}, u32[]{:S(2)}) collective-permute-start(bf16[1,384,4096]{2,1,0:T(8,128)(2,1)} %param.13), channel_id=1, source_target_pairs={{0,1},{1,0},{2,3},{3,2},{4,5},{5,4},{6,7},{7,6},{8,9},{9,8},{10,11... | collective-permute-start | bytes 9437192 | tf_op jit(solution)/shard_map/ppermute | solution.py:197
